TPU v7x, 32 devices: a whole 2x2x4 slice. The times are simulated.
32 devices in a mesh: tm: 4 (over y, x), rows: 4 (over z), clip: 2 (over core).
Axes of the slice: x: 2, y: 2, z: 4, core: 2. Of those that a mesh axis runs over, the one named last changes fastest.
Arguments:
- features: bfloat16 [8, 16, 8, 9984], P('clip', 'tm', 'rows'), may hold values from -6 to 6
- lengths: int32 [8], replicated, may hold values from 1 to 16, as said below
- stored_slot: int32 [8], replicated, may hold values from 0 to 7, each once
- owner_slot: int32 [8], replicated, may hold values from 0 to 7, each once
- gain_first: float32 [96], replicated, may hold values from 0.1 to 1.9
- conv_first: bfloat16 [3, 3, 3, 96, 96], replicated, may hold values from -0.125 to 0.125
- bias_first: float32 [96], replicated, may hold values from -3 to 3
- gain_second: float32 [96], replicated, may hold values from 0.1 to 1.9
- conv_second: bfloat16 [3, 3, 3, 96, 96], replicated, may hold values from -0.125 to 0.125
- bias_second: float32 [96], replicated, may hold values from -3 to 3
- reduce_conv_weight: bfloat16 [3, 3, 96, 96], replicated, may hold values from -0.21875 to 0.21875
- reduce_conv_bias: float32 [96], replicated, may hold values from -3 to 3
Outputs:
- encoded: bfloat16 [8, 16, 4, 4992], P('clip', 'tm', 'rows')
Inputs may be any that keep to these rules, and one draw needn't show every extreme that they name: `lengths`: some clip has all 16 frames. `stored_slot`: each clip has its own storage slot. `owner_slot`: each clip has its own output slot.
All inputs are finite; a program needn't handle non-finite values.
Results may differ from a plain program's by a relative error of at most 0.0051.
Values may be sent and summed in bfloat16 or wider, within the bound.
No kernel may reach another device: no remote copies, remote signals or barrier semaphores. Data moves between devices by JAX's collectives and lax.ppermute only.
A program may use at most 64 MiB of HBM per device.

v0:
```python
import functools

import jax
import jax.numpy as jnp
from jax import lax
from jax.experimental import pallas as pl
from jax.experimental.pallas import tpu as pltpu
from jax.sharding import PartitionSpec as P

NORM_EPS = 1e-06
LANES = 128
LEFT, RIGHT = 2, 4


def from_behind(value, axis, steps):
    count = lax.axis_size(axis)
    first, last = (max(0, -steps), min(count, count - steps))
    return lax.ppermute(value, axis, [(source, source + steps) for source in range(first, last)])


def padded_2(x, sides, width):
    for axis, dim in sides:
        count, length = (lax.axis_size(axis), x.shape[dim])
        up = [(i, (i + 1) % count) for i in range(count - 1)]
        down = [(j, i) for i, j in up]
        last = lax.slice_in_dim(x, length - width, length, axis=dim)
        first = lax.slice_in_dim(x, 0, width, axis=dim)
        before = lax.ppermute(last, axis, up)
        after = lax.ppermute(first, axis, down)
        x = jnp.concatenate([before, x, after], axis=dim)
    return x


def norm_silu(values, gain_vec):
    scaled = (
        values * lax.rsqrt(jnp.mean(values * values, axis=-1, keepdims=True) + NORM_EPS) * gain_vec
    )
    return jax.nn.silu(scaled)


def conv_valid(grown_block, kernel_weight, bias_vector):
    batch = grown_block.shape[0]
    frames = grown_block.shape[1] - 2
    band_rows = grown_block.shape[2] - 2
    columns = grown_block.shape[3]
    channels = grown_block.shape[4]
    outputs = kernel_weight.shape[4]
    padded = jnp.pad(grown_block, ((0, 0), (0, 0), (0, 0), (1, 1), (0, 0)))
    running_sum = jnp.zeros((batch * frames * band_rows * columns, outputs), jnp.float32)
    for step_t in range(3):
        for step_h in range(3):
            window = padded[:, step_t : step_t + frames, step_h : step_h + band_rows]
            tap_stack = jnp.concatenate(
                [window[:, :, :, step_w : step_w + columns] for step_w in range(3)], axis=-1
            )
            running_sum = running_sum + jnp.dot(
                tap_stack.reshape(-1, 3 * channels),
                kernel_weight[step_t, step_h].reshape(3 * channels, outputs),
                preferred_element_type=jnp.float32,
            )
    return (running_sum + bias_vector).reshape(batch, frames, band_rows, columns, outputs)


def spatial_reduce(padded_frames, kernel_weight, bias_vector):
    batch = padded_frames.shape[0]
    frames = padded_frames.shape[1]
    half_rows = (padded_frames.shape[2] - 1) // 2
    columns = padded_frames.shape[3]
    channels = padded_frames.shape[4]
    outputs = kernel_weight.shape[3]
    padded = jnp.pad(padded_frames, ((0, 0), (0, 0), (0, 0), (0, 1), (0, 0)))
    running_sum = jnp.zeros((batch * frames * half_rows * (columns // 2), outputs), jnp.float32)
    for step_h in range(3):
        row_band = padded[:, :, step_h : step_h + 2 * half_rows - 1 : 2]
        tap_stack = jnp.concatenate(
            [row_band[:, :, :, step_w : step_w + columns - 1 : 2] for step_w in range(3)], axis=-1
        )
        running_sum = running_sum + jnp.dot(
            tap_stack.reshape(-1, 3 * channels),
            kernel_weight[step_h].reshape(3 * channels, outputs),
            preferred_element_type=jnp.float32,
        )
    return (running_sum + bias_vector).reshape(batch, frames, half_rows, columns // 2, outputs)


def encode(
    clip_block,
    length,
    gain_first,
    conv_first,
    bias_first,
    gain_second,
    conv_second,
    bias_second,
    reduce_conv_weight,
    reduce_conv_bias,
):
    batch = clip_block.shape[0]
    frames = clip_block.shape[1]
    band_rows = clip_block.shape[2]
    channels = gain_first.shape[0]
    columns = clip_block.shape[3] // channels
    feature_map = clip_block.reshape(batch, frames, band_rows, columns, channels)
    first_frame = lax.axis_index("tm") * frames
    first_act = norm_silu(feature_map.astype(jnp.float32), gain_first).astype(jnp.bfloat16)
    earlier = from_behind(first_act[:, frames - 2 :], "tm", 1)
    grown_block = padded_2(jnp.concatenate([earlier, first_act], axis=1), (("rows", 2),), 1)
    first_conv = conv_valid(grown_block, conv_first, bias_first)
    second_act = norm_silu(first_conv, gain_second).astype(jnp.bfloat16)
    earlier_two = from_behind(second_act[:, frames - 2 :], "tm", 1)
    grown_two = padded_2(jnp.concatenate([earlier_two, second_act], axis=1), (("rows", 2),), 1)
    branch = conv_valid(grown_two, conv_second, bias_second)
    residual_block_output = (feature_map.astype(jnp.float32) + branch).astype(jnp.bfloat16)
    lower_neighbor_row = from_behind(residual_block_output[:, :, :1], "rows", -1)
    spatial_reduced = spatial_reduce(
        jnp.concatenate([residual_block_output, lower_neighbor_row], axis=2),
        reduce_conv_weight,
        reduce_conv_bias,
    )
    alive_frame = (first_frame + jnp.arange(frames, dtype=jnp.int32))[None, :] < length[:, None]
    masked = jnp.where(alive_frame[:, :, None, None, None], spatial_reduced, 0.0).astype(
        jnp.bfloat16
    )
    return masked.reshape(batch, frames, band_rows // 2, columns // 2 * channels)


def general_local(
    features,
    lengths,
    stored_slot,
    owner_slot,
    gain_first,
    conv_first,
    bias_first,
    gain_second,
    conv_second,
    bias_second,
    reduce_conv_weight,
    reduce_conv_bias,
):
    local_count = features.shape[0]
    my_slots = lax.axis_index("clip") * local_count + jnp.arange(local_count, dtype=jnp.int32)
    numbers = jnp.arange(stored_slot.shape[0], dtype=jnp.int32)
    placed = (stored_slot[:, None] == numbers[None, :]).astype(jnp.int32)
    target = jnp.sum(placed * owner_slot[:, None], axis=0)
    hits = (stored_slot[None, :] == my_slots[:, None]).astype(jnp.int32)
    length = jnp.sum(hits * lengths[None, :], axis=1)
    local_out = encode(
        features,
        length,
        gain_first,
        conv_first,
        bias_first,
        gain_second,
        conv_second,
        bias_second,
        reduce_conv_weight,
        reduce_conv_bias,
    )
    shard_piece = lax.all_gather(local_out, "clip", axis=0, tiled=True)
    sources = jnp.arange(shard_piece.shape[0], dtype=jnp.int32)
    source_hits = (sources[:, None] == numbers[None, :]).astype(jnp.int32)
    goes_to = jnp.sum(source_hits * target[None, :], axis=1)
    weights = (goes_to[None, :] == my_slots[:, None]).astype(shard_piece.dtype)
    return jnp.einsum(
        "ki,iabc->kabc", weights, shard_piece, preferred_element_type=jnp.float32
    ).astype(shard_piece.dtype)


class Plan:
    def __init__(self, mesh, features, channels):
        self.blocks, self.bands, self.cores = (mesh.shape[a] for a in ("tm", "rows", "clip"))
        self.clips = features.shape[0] // self.cores
        self.frames = features.shape[1] // self.blocks
        self.band = features.shape[2] // self.bands
        self.all_frames, self.height = features.shape[1], features.shape[2]
        self.channels = channels
        self.width = features.shape[3] // channels
        self.parts = self.blocks
        self.own = self.width // self.parts
        self.window = self.own + LEFT + RIGHT
        self.pairs = self.window // 2
        self.devices = self.blocks * self.bands

    def fits(self):
        return (
            self.bands == self.clips
            and self.width % (2 * self.parts) == 0
            and self.channels <= LANES
            and self.band == 2
            and self.band * self.frames == 8
            and self.all_frames == 16
            and (self.window * self.channels) % LANES == 0
        )


def lanes_of(shape):
    return lax.broadcasted_iota(jnp.int32, shape, len(shape) - 1)


def spread_columns(plan, dense, column):
    start = column * plan.channels
    first, off = start // LANES * LANES, start % LANES
    value = dense[:, first : first + LANES]
    if off + plan.channels > LANES:
        following = dense[:, first + LANES : first + 2 * LANES]
        value = jnp.where(lanes_of(value.shape) >= off, value, following)
    if off:
        value = pltpu.roll(value, LANES - off, 1)
    return jnp.where(lanes_of(value.shape) < plan.channels, value, 0.0)


def merge_columns(plan, columns):
    rows = columns[0].shape[0]
    total = -(-len(columns) * plan.channels // LANES)
    merged = [None] * total
    for index, value in enumerate(columns):
        start = index * plan.channels
        first, off = start // LANES, start % LANES
        turned = pltpu.roll(value, off, 1) if off else value
        lane = lanes_of((rows, LANES))
        merged[first] = turned if off == 0 else jnp.where(lane >= off, turned, merged[first])
        if off + plan.channels > LANES:
            merged[first + 1] = turned
    return merged


def encode_kernel(
    plan,
    lengths_ref,
    stored_ref,
    pieces_ref,
    gain_first_ref,
    weight_first_ref,
    bias_first_ref,
    gain_second_ref,
    weight_second_ref,
    bias_second_ref,
    weight_reduce_ref,
    bias_reduce_ref,
    out_ref,
    x_ref,
    act_ref,
    conv_ref,
    block_ref,
    big_ref,
    big_reduce_ref,
    vector_ref,
):
    frames, height, pairs, channels = plan.all_frames, plan.height, plan.pairs, plan.channels
    rows = height * frames
    part = lax.axis_index("tm")
    slot = lax.axis_index("clip") * plan.clips + lax.axis_index("rows")

    vector_ref[...] = jnp.zeros_like(vector_ref)
    for row, ref in enumerate(
        (gain_first_ref, bias_first_ref, gain_second_ref, bias_second_ref, bias_reduce_ref)
    ):
        vector_ref[row : row + 1, 0:channels] = ref[...]

    half = plan.frames
    sublane = lax.broadcasted_iota(jnp.int32, (8, LANES), 0)
    for band in range(plan.bands):
        dense = [
            pieces_ref[block * plan.bands + band].astype(jnp.float32)
            for block in range(plan.blocks)
        ]
        for column in range(plan.window):
            spread = [spread_columns(plan, piece, column) for piece in dense]
            turned = [pltpu.roll(value, half, 0) for value in spread]
            upper = [
                jnp.where(sublane < half, spread[2 * i], turned[2 * i + 1])
                for i in range(len(spread) // 2)
            ]
            lower = [
                jnp.where(sublane < half, turned[2 * i], spread[2 * i + 1])
                for i in range(len(spread) // 2)
            ]
            x_ref[column, 2 * band] = jnp.concatenate(upper, axis=0)
            x_ref[column, 2 * band + 1] = jnp.concatenate(lower, axis=0)

    def sum_matrix():
        shape = (2 * LANES, 2 * LANES)
        across = lax.broadcasted_iota(jnp.int32, shape, 0) // LANES
        along = lax.broadcasted_iota(jnp.int32, shape, 1) // LANES
        return jnp.where(across == along, 1.0, 0.0).astype(jnp.bfloat16)

    ones = sum_matrix()
    frame_of_row = lax.broadcasted_iota(jnp.int32, (rows, 2 * LANES), 0) % frames

    def in_image(pair):
        lane = lax.broadcasted_iota(jnp.int32, (1, 2 * LANES), 1)
        column = part * plan.own - LEFT + 2 * pair + lane // LANES
        return (column >= 0) & (column < plan.width)

    def activate(pair, values, gain):
        squares = (values * values).astype(jnp.bfloat16)
        sums = jnp.dot(squares, ones, preferred_element_type=jnp.float32)
        scale = jnp.where(in_image(pair), gain * (0.5 * channels**0.5), 0.0)
        scaled = values * lax.rsqrt(sums + channels * NORM_EPS) * scale
        act = scaled + scaled * jnp.tanh(scaled)
        for shift in range(3):
            moved = act
            if shift:
                moved = jnp.where(frame_of_row >= shift, pltpu.roll(act, shift, 0), 0.0)
            moved = moved.astype(jnp.bfloat16)
            for side in range(2):
                act_ref[2 - shift, 2 * pair + side + 1, 1 : height + 1] = moved[
                    :, side * LANES : (side + 1) * LANES
                ].reshape(height, frames, LANES)

    def both(row):
        vector = vector_ref[row : row + 1, :]
        return jnp.concatenate([vector, vector], axis=1)

    def spread_weights(weight_ref):
        big_ref[...] = jnp.zeros_like(big_ref)
        for tap in range(9):
            for side in range(2):
                for step in range(3):
                    first = (tap * 4 + side + step) * LANES
                    big_ref[
                        first : first + channels, side * LANES : side * LANES + channels
                    ] = weight_ref[tap * 3 + step]

    def convolve(first_pair, count):
        parts = []
        for tap in range(9):
            step_t, step_h = tap // 3, tap % 3
            for step in range(4):
                parts.append(
                    jnp.concatenate(
                        [
                            act_ref[
                                step_t, 2 * (first_pair + i) + step, step_h : step_h + height
                            ].reshape(rows, LANES)
                            for i in range(count)
                        ],
                        axis=0,
                    )
                )
        stack = jnp.concatenate(parts, axis=1)
        return jnp.dot(stack, big_ref[...], preferred_element_type=jnp.float32)

    act_ref[:, :, 0] = jnp.zeros_like(act_ref[:, :, 0])
    act_ref[:, :, height + 1] = jnp.zeros_like(act_ref[:, :, height + 1])
    act_ref[:, 0] = jnp.zeros_like(act_ref[:, 0])

    gain_first, gain_second = both(0), both(2)
    bias_first, bias_second = both(1), both(3)

    spread_weights(weight_first_ref)

    @pl.loop(0, pairs)
    def _(pair):
        values = jnp.concatenate(
            [x_ref[2 * pair + side].reshape(rows, LANES) for side in range(2)], axis=1
        )
        activate(pair, values, gain_first)

    group = 3

    @pl.loop(0, (pairs - 1) // group)
    def _(step):
        result = convolve(step * group, group) + bias_first
        for i in range(group):
            conv_ref[step * group + i] = result[i * rows : (i + 1) * rows]

    spread_weights(weight_second_ref)

    @pl.loop(0, pairs - 1)
    def _(pair):
        activate(pair, conv_ref[pair], gain_second)

    block_ref[:, height] = jnp.zeros_like(block_ref[:, height])
    pair_count = 2

    @pl.loop(0, (pairs - 2) // pair_count)
    def _(step):
        result = convolve(1 + step * pair_count, pair_count) + bias_second
        for i in range(pair_count):
            pair = 1 + step * pair_count + i
            for side in range(2):
                value = result[i * rows : (i + 1) * rows, side * LANES : (side + 1) * LANES]
                value = value.reshape(height, frames, LANES) + x_ref[2 * pair + side]
                column = part * plan.own - LEFT + 2 * pair + side
                value = jnp.where((column >= 0) & (column < plan.width), value, 0.0)
                block_ref[2 * pair + side, 0:height] = value.astype(jnp.bfloat16)

    big_reduce_ref[...] = jnp.zeros_like(big_reduce_ref)
    for tap in range(9):
        big_reduce_ref[tap * LANES : tap * LANES + channels, 0:channels] = weight_reduce_ref[tap]

    length = jnp.int32(0)
    for clip in range(lengths_ref.shape[0]):
        length = length + jnp.where(stored_ref[clip] == slot, lengths_ref[clip], 0)

    outputs, half_rows = plan.own // 2, height // 2
    columns = []
    for j in range(outputs):
        parts = []
        for tap in range(9):
            step_h, step_w = tap // 3, tap % 3
            parts.append(
                jnp.concatenate(
                    [block_ref[LEFT + 2 * j + step_w, 2 * i + step_h] for i in range(half_rows)],
                    axis=0,
                )
            )
        stack = jnp.concatenate(parts, axis=1)
        columns.append(stack)
    stack = jnp.concatenate(columns, axis=0)
    reduced = jnp.dot(stack, big_reduce_ref[...], preferred_element_type=jnp.float32)
    reduced = reduced + vector_ref[4:5, :]
    alive = lax.broadcasted_iota(jnp.int32, (half_rows * frames, LANES), 0) % frames < length
    size = half_rows * frames
    merged = merge_columns(
        plan, [jnp.where(alive, reduced[j * size : (j + 1) * size], 0.0) for j in range(outputs)]
    )
    for tile, value in enumerate(merged):
        for i in range(half_rows):
            for block in range(plan.blocks):
                first = i * frames + block * plan.frames
                out_ref[block * plan.bands + i, :, tile * LANES : (tile + 1) * LANES] = value[
                    first : first + plan.frames
                ].astype(jnp.bfloat16)


def encode_window(
    plan, pieces, lengths, stored_slot, gain_first, conv_first, bias_first, gain_second,
    conv_second, bias_second, reduce_conv_weight, reduce_conv_bias,
):
    channels, pairs = plan.channels, plan.pairs
    rows = plan.height * plan.all_frames
    out_tiles = -(-plan.own // 2 * channels // LANES)
    vmem = pl.BlockSpec(memory_space=pltpu.VMEM)
    smem = pl.BlockSpec(memory_space=pltpu.SMEM)
    return pl.pallas_call(
        functools.partial(encode_kernel, plan),
        out_shape=jax.ShapeDtypeStruct(
            (plan.devices, plan.frames, out_tiles * LANES), jnp.bfloat16
        ),
        in_specs=[smem, smem] + [vmem] * 9,
        out_specs=vmem,
        scratch_shapes=[
            pltpu.VMEM((plan.window, plan.height, plan.all_frames, LANES), jnp.float32),
            pltpu.VMEM((3, plan.window + 2, plan.height + 2, plan.all_frames, LANES), jnp.bfloat16),
            pltpu.VMEM((pairs, rows, 2 * LANES), jnp.float32),
            pltpu.VMEM((plan.window, plan.height + 1, plan.all_frames, LANES), jnp.bfloat16),
            pltpu.VMEM((9 * 4 * LANES, 2 * LANES), jnp.bfloat16),
            pltpu.VMEM((9 * LANES, LANES), jnp.bfloat16),
            pltpu.VMEM((8, LANES), jnp.float32),
        ],
        compiler_params=pltpu.CompilerParams(vmem_limit_bytes=48 * 2**20),
    )(
        lengths,
        stored_slot,
        pieces,
        gain_first.reshape(1, channels),
        conv_first.reshape(27, channels, channels),
        bias_first.reshape(1, channels),
        gain_second.reshape(1, channels),
        conv_second.reshape(27, channels, channels),
        bias_second.reshape(1, channels),
        reduce_conv_weight.reshape(9, channels, channels),
        reduce_conv_bias.reshape(1, channels),
    )


def window_local(
    plan, features, lengths, stored_slot, owner_slot, gain_first, conv_first, bias_first,
    gain_second, conv_second, bias_second, reduce_conv_weight, reduce_conv_bias,
):
    channels, clips, parts = plan.channels, plan.clips, plan.parts
    piece_rows = plan.frames * plan.band
    dense = features.transpose(0, 2, 1, 3).reshape(clips, piece_rows, -1)
    dense = jnp.pad(dense, ((0, 0), (0, 0), (LEFT * channels, RIGHT * channels)))
    pieces = jnp.concatenate(
        [
            dense[:, :, q * plan.own * channels :][:, :, : plan.window * channels]
            for q in range(parts)
        ],
        axis=0,
    )
    pieces = lax.all_to_all(pieces, ("tm", "rows"), 0, 0, tiled=True)
    out = encode_window(
        plan, pieces, lengths, stored_slot, gain_first, conv_first, bias_first, gain_second,
        conv_second, bias_second, reduce_conv_weight, reduce_conv_bias,
    )
    out = lax.all_to_all(out, ("tm", "rows"), 0, 0, tiled=True)
    used = plan.own // 2 * channels
    out = out[:, :, :used].reshape(parts, clips, plan.frames, used)
    out = out.transpose(1, 2, 0, 3).reshape(clips, plan.frames, 1, parts * used)
    both = lax.all_gather(out, "clip", axis=0, tiled=True)
    numbers = jnp.arange(stored_slot.shape[0], dtype=jnp.int32)
    my_slots = lax.axis_index("clip") * clips + numbers[:clips]
    wanted = (owner_slot[None, :] == my_slots[:, None]).astype(jnp.int32)
    source = jnp.sum(wanted * stored_slot[None, :], axis=1)
    weights = (source[:, None] == numbers[None, :]).astype(out.dtype)
    return jnp.einsum(
        "ki,iabc->kabc", weights, both, preferred_element_type=jnp.float32
    ).astype(out.dtype)


def solution(mesh):
    out_specs = P("clip", "tm", "rows", None)
    in_specs = (out_specs,) + (P(),) * 11

    def run(features, *others):
        plan = Plan(mesh, features, others[3].shape[0])
        inner = functools.partial(window_local, plan) if plan.fits() else general_local
        return jax.shard_map(
            inner, mesh=mesh, in_specs=in_specs, out_specs=out_specs, check_vma=False
        )(features, *others)

    return run
```

profile of v0, /device:TPU:0, one launch (start us, length us, event | category | flops | bytes accessed | tf_op | source)
XLA Modules:
  0.0 70.0 jit_solution(7440895104520414009)
XLA Ops:
  0.0 1.3 %copy.20 = bf16[4,2,4,9984]{3,2,1,0:T(4,128)(2,1)S(1)} copy(bf16[4,2,4,9984]{3,1,2,0:T(2,128)(2,1)} %bitcast.30) | data formatting | bytes 1277952 | tf_op jit(solution)/shard_map/transpose | solution.py:476
  1.3 0.1 reshape.42
  1.5 0.2 pad_slice_fusion.1
  1.7 1.0 %pad_maximum_fusion = bf16[16,8,3072]{2,1,0:T(8,128)(2,1)} fusion(bf16[4,8,3072]{2,1,0:T(8,128)(2,1)S(1)} %get-tuple-element.6, bf16[4,8,3072]{2,1,0:T(8,128)(2,1)S(1)} %get-tuple-element.7, bf16[4,8,3072]{2,1,0:T(8,128)(2,1)S(1)} %get-tuple-element.8, bf16[4,8,3072]{2,1,0:T(8,128)(2,1)S(1)} %get-tuple-element.5), kind=kLoop, calls=%fused_computation.2 | loop fusion | flops 1179648 | bytes 1572864 | tf_op jit(solution)/shard_map/concatenate | solution.py:478
  2.7 0.0 copy-start
  2.7 0.0 copy-start.1
  2.7 0.0 copy-start.2
  2.7 0.0 copy-start.6
  2.7 0.0 copy-start.7
  2.7 0.0 copy-start.8
  2.7 0.0 copy-start.9
  2.7 8.5 %all-to-all-start = ((bf16[16,8,3072]{2,1,0:T(8,128)(2,1)}), bf16[16,8,3072]{2,1,0:T(8,128)(2,1)S(1)}, u32[]{:S(2)}, u32[]{:S(2)}) async-start(bf16[16,8,3072]{2,1,0:T(8,128)(2,1)} %pad_maximum_fusion), calls=%async_computation | async-start | bytes 1572864 | tf_op jit(solution)/shard_map/all_to_all | solution.py:485
  11.2 21.8 %all-to-all-done.pieces_ref = bf16[16,8,3072]{2,1,0:T(8,128)(2,1)S(1)} async-done(((bf16[16,8,3072]{2,1,0:T(8,128)(2,1)}), bf16[16,8,3072]{2,1,0:T(8,128)(2,1)S(1)}, u32[]{:S(2)}, u32[]{:S(2)}) %all-to-all-start) | async-done | bytes 786464 | tf_op jit(solution)/shard_map/all_to_all | solution.py:485
  33.0 0.0 copy-start.3
  33.0 0.0 copy-start.4
  33.0 0.0 copy-start.5
  33.0 0.0 copy-done
  33.0 0.0 copy-done.1
  33.1 0.0 copy-done.2
  33.1 0.0 copy-done.6
  33.1 0.0 copy-done.7
  33.1 0.0 copy-done.8
  33.1 0.0 copy-done.9
  33.1 0.6 copy-done.3
  33.7 0.0 copy-done.4
  33.7 0.0 copy-done.5
  33.7 21.5 %shard_map.118 = bf16[16,4,1280]{2,1,0:T(4,128)(2,1)} custom-call(s32[8]{0:T(128)S(1)} %copy-done.4, s32[8]{0:T(128)S(1)} %copy-done.3, bf16[16,8,3072]{2,1,0:T(8,128)(2,1)S(1)} %all-to-all-done.pieces_ref, f32[1,96]{1,0:T(1,128)S(1)} %bitcast.24, bf16[27,96,96]{2,1,0:T(8,128)(2,1)S(1)} %bitcast.21, f32[1,96]{1,0:T(1,128)S(1)} %bitcast.25, ...), custom_call_target="tpu_custom_call" | custom-call | tf_op jit(solution)/shard_map/pallas_call | solution.py:438
  55.2 3.5 %all-to-all-start.1 = ((bf16[16,4,1280]{2,1,0:T(4,128)(2,1)}), bf16[16,4,1280]{2,1,0:T(4,128)(2,1)S(1)}, u32[]{:S(2)}, u32[]{:S(2)}) async-start(bf16[16,4,1280]{2,1,0:T(4,128)(2,1)} %shard_map.118), calls=%async_computation.1 | async-start | bytes 327680 | tf_op jit(solution)/shard_map/all_to_all | solution.py:490
  58.7 0.0 copy-start.10
  58.8 0.6 copy-done.10
  59.4 0.2 select_reduce_fusion
  59.6 7.1 %all-to-all-done.1 = bf16[16,4,1280]{2,1,0:T(4,128)(2,1)S(1)} async-done(((bf16[16,4,1280]{2,1,0:T(4,128)(2,1)}), bf16[16,4,1280]{2,1,0:T(4,128)(2,1)S(1)}, u32[]{:S(2)}, u32[]{:S(2)}) %all-to-all-start.1) | async-done | bytes 163872 | tf_op jit(solution)/shard_map/all_to_all | solution.py:490
  66.7 0.1 copy.21
  66.8 0.2 reshape.52
  67.0 2.0 %all_gather.3 = bf16[8,4,1,4992]{3,1,2,0:T(4,128)(2,1)S(1)} all-gather(bf16[4,4,1,4992]{3,1,2,0:T(4,128)(2,1)S(1)} %reshape.52), channel_id=1, replica_groups=mesh['tm'=4,'rows'=4,'clip'=2] {'clip'}, dimensions={0}, use_global_device_ids=true | all-gather | bytes 479232 | tf_op jit(solution)/shard_map/all_gather | solution.py:494
  69.0 0.3 fusion
  69.3 0.7 %copy.23 = bf16[4,4,1,4992]{3,1,2,0:T(4,128)(2,1)} copy(bf16[4,4,1,4992]{3,0,1,2:T(4,128)(2,1)S(1)} %fusion) | data formatting | bytes 319488 | tf_op jit(solution)/shard_map/convert_element_type | solution.py:502
  (2 shorter events, 0.0 us)
Async XLA Ops:
  2.7 30.4 %copy-start = (bf16[3,3,3,96,96]{4,3,2,1,0:T(8,128)(2,1)S(1)}, bf16[3,3,3,96,96]{4,3,2,1,0:T(8,128)(2,1)}, u32[]{:S(2)}) copy-start(bf16[3,3,3,96,96]{4,3,2,1,0:T(8,128)(2,1)} %param.17) | copy-start | bytes 1492996
  2.7 30.4 %copy-start.1 = (bf16[3,3,3,96,96]{4,3,2,1,0:T(8,128)(2,1)S(1)}, bf16[3,3,3,96,96]{4,3,2,1,0:T(8,128)(2,1)}, u32[]{:S(2)}) copy-start(bf16[3,3,3,96,96]{4,3,2,1,0:T(8,128)(2,1)} %param.20) | copy-start | bytes 1492996
  2.7 30.4 %copy-start.2 = (bf16[3,3,96,96]{3,2,1,0:T(8,128)(2,1)S(1)}, bf16[3,3,96,96]{3,2,1,0:T(8,128)(2,1)}, u32[]{:S(2)}) copy-start(bf16[3,3,96,96]{3,2,1,0:T(8,128)(2,1)} %param.22) | copy-start | bytes 497668
  2.7 30.4 %copy-start.6 = (f32[96]{0:T(128)S(1)}, f32[96]{0:T(128)}, u32[]{:S(2)}) copy-start(f32[96]{0:T(128)} %param.18) | copy-start | bytes 1156
  2.7 30.4 %copy-start.7 = (f32[96]{0:T(128)S(1)}, f32[96]{0:T(128)}, u32[]{:S(2)}) copy-start(f32[96]{0:T(128)} %param.19) | copy-start | bytes 1156
  2.7 30.4 %copy-start.8 = (f32[96]{0:T(128)S(1)}, f32[96]{0:T(128)}, u32[]{:S(2)}) copy-start(f32[96]{0:T(128)} %param.21) | copy-start | bytes 1156
  2.7 30.4 %copy-start.9 = (f32[96]{0:T(128)S(1)}, f32[96]{0:T(128)}, u32[]{:S(2)}) copy-start(f32[96]{0:T(128)} %param.23) | copy-start | bytes 1156
  2.7 30.3 %all-to-all-start = ((bf16[16,8,3072]{2,1,0:T(8,128)(2,1)}), bf16[16,8,3072]{2,1,0:T(8,128)(2,1)S(1)}, u32[]{:S(2)}, u32[]{:S(2)}) async-start(bf16[16,8,3072]{2,1,0:T(8,128)(2,1)} %pad_maximum_fusion), calls=%async_computation | async-start | bytes 1572864 | tf_op jit(solution)/shard_map/all_to_all | solution.py:485
  33.0 0.7 copy-start.3
  33.0 0.7 copy-start.4
  33.0 0.7 copy-start.5
  55.2 11.5 %all-to-all-start.1 = ((bf16[16,4,1280]{2,1,0:T(4,128)(2,1)}), bf16[16,4,1280]{2,1,0:T(4,128)(2,1)S(1)}, u32[]{:S(2)}, u32[]{:S(2)}) async-start(bf16[16,4,1280]{2,1,0:T(4,128)(2,1)} %shard_map.118), calls=%async_computation.1 | async-start | bytes 327680 | tf_op jit(solution)/shard_map/all_to_all | solution.py:490
  58.7 0.7 copy-start.10
where the time goes:
time: 70.4 us; the launch traced here: 70 us
  waiting for transfers between devices  29 us (41%)
  Pallas kernels  21.5 us (31%)
  starting transfers between devices  12 us (17%)
  local copies, waits for them, and re-layouts  3.94 us (6%)
  blocking collectives  2.04 us (3%)
  other arithmetic  1.19 us (2%)
    all_to_all x1, waiting for transfers between devices, window_local(): pieces = lax.all_to_all(pieces, ('tm', 'rows'), 0, 0, tiled=True)  21.8 us
    pallas_call x1, Pallas kernels, encode_window(): pl.pallas_call(functools.partial(encode_kernel, plan), out_shape=jax.Shap...  21.5 us
    all_to_all x1, starting transfers between devices, window_local(): pieces = lax.all_to_all(pieces, ('tm', 'rows'), 0, 0, tiled=True)  8.46 us
    all_to_all x1, waiting for transfers between devices, window_local(): out = lax.all_to_all(out, ('tm', 'rows'), 0, 0, tiled=True)  7.13 us
    all_to_all x1, starting transfers between devices, window_local(): out = lax.all_to_all(out, ('tm', 'rows'), 0, 0, tiled=True)  3.52 us
    all_gather x1, blocking collectives, window_local(): both = lax.all_gather(out, 'clip', axis=0, tiled=True)  2.04 us
  transfers between devices with their start and end apart: 2, of which 2 were waited for; matrix products, arithmetic and copies ran while one was open for 0% of the time, Pallas kernels for 0%

commit v1 on v0

--- a/solution.py
+++ b/solution.py
@@ -167,6 +167,9 @@
     ).astype(shard_piece.dtype)
 
 
+CHUNKS = 4
+
+
 class Plan:
     def __init__(self, mesh, features, channels):
         self.blocks, self.bands, self.cores = (mesh.shape[a] for a in ("tm", "rows", "clip"))
@@ -186,7 +189,7 @@
         return (
             self.bands == self.clips
             and self.width % (2 * self.parts) == 0
-            and self.channels <= LANES
+            and 3 * (LANES - self.channels) == self.channels
             and self.band == 2
             and self.band * self.frames == 8
             and self.all_frames == 16
@@ -225,26 +228,71 @@
     return merged
 
 
+def weights_kernel(plan, first_ref, second_ref, reduce_ref, big_first_ref, big_second_ref, big_reduce_ref):
+    channels = plan.channels
+    spare = LANES - channels
+    for weight_ref, big_ref in ((first_ref, big_first_ref), (second_ref, big_second_ref)):
+        big_ref[...] = jnp.zeros_like(big_ref)
+        for tap in range(9):
+            for side in range(2):
+                for step in range(3):
+                    tile = side + step
+                    along = pl.ds(side * LANES, channels)
+                    if tile < 3:
+                        first = (tap * 3 + tile) * LANES
+                        big_ref[first : first + channels, along] = weight_ref[tap * 3 + step]
+                        continue
+                    for tile in range(3):
+                        first = (tap * 3 + tile) * LANES + channels
+                        big_ref[first : first + spare, along] = weight_ref[
+                            tap * 3 + step, tile * spare : (tile + 1) * spare
+                        ]
+    big_reduce_ref[...] = jnp.zeros_like(big_reduce_ref)
+    for tap in range(9):
+        big_reduce_ref[tap * LANES : tap * LANES + channels, 0:channels] = reduce_ref[tap]
+
+
+def spread_weights(plan, conv_first, conv_second, reduce_conv_weight):
+    channels = plan.channels
+    vmem = pl.BlockSpec(memory_space=pltpu.VMEM)
+    conv = jax.ShapeDtypeStruct((9 * 3 * LANES, 2 * LANES), jnp.bfloat16)
+    reduction = jax.ShapeDtypeStruct((9 * LANES, LANES), jnp.bfloat16)
+    return pl.pallas_call(
+        functools.partial(weights_kernel, plan),
+        out_shape=(conv, conv, reduction),
+        in_specs=[vmem] * 3,
+        out_specs=(vmem,) * 3,
+        compiler_params=pltpu.CompilerParams(vmem_limit_bytes=16 * 2**20),
+        cost_estimate=pl.CostEstimate(flops=0, transcendentals=0, bytes_accessed=6 * 2**20),
+    )(
+        conv_first.reshape(27, channels, channels),
+        conv_second.reshape(27, channels, channels),
+        reduce_conv_weight.reshape(9, channels, channels),
+    )
+
+
 def encode_kernel(
     plan,
     lengths_ref,
     stored_ref,
     pieces_ref,
     gain_first_ref,
-    weight_first_ref,
+    big_first_ref,
     bias_first_ref,
     gain_second_ref,
-    weight_second_ref,
+    big_second_ref,
     bias_second_ref,
-    weight_reduce_ref,
+    big_reduce_ref,
     bias_reduce_ref,
     out_ref,
     x_ref,
-    act_ref,
+    act_first_ref,
+    act_second_ref,
+    wide_first_ref,
+    wide_second_ref,
     conv_ref,
     block_ref,
-    big_ref,
-    big_reduce_ref,
+    reduced_ref,
     vector_ref,
 ):
     frames, height, pairs, channels = plan.all_frames, plan.height, plan.pairs, plan.channels
@@ -286,100 +334,86 @@
         return jnp.where(across == along, 1.0, 0.0).astype(jnp.bfloat16)
 
     ones = sum_matrix()
-    frame_of_row = lax.broadcasted_iota(jnp.int32, (rows, 2 * LANES), 0) % frames
+    frame_of_row = lax.broadcasted_iota(jnp.int32, (rows, LANES), 0) % frames
 
     def in_image(pair):
         lane = lax.broadcasted_iota(jnp.int32, (1, 2 * LANES), 1)
         column = part * plan.own - LEFT + 2 * pair + lane // LANES
         return (column >= 0) & (column < plan.width)
 
-    def activate(pair, values, gain):
+    def activate(wide_ref, pair, values, gain):
         squares = (values * values).astype(jnp.bfloat16)
         sums = jnp.dot(squares, ones, preferred_element_type=jnp.float32)
         scale = jnp.where(in_image(pair), gain * (0.5 * channels**0.5), 0.0)
         scaled = values * lax.rsqrt(sums + channels * NORM_EPS) * scale
-        act = scaled + scaled * jnp.tanh(scaled)
-        for shift in range(3):
-            moved = act
-            if shift:
-                moved = jnp.where(frame_of_row >= shift, pltpu.roll(act, shift, 0), 0.0)
-            moved = moved.astype(jnp.bfloat16)
-            for side in range(2):
-                act_ref[2 - shift, 2 * pair + side + 1, 1 : height + 1] = moved[
-                    :, side * LANES : (side + 1) * LANES
-                ].reshape(height, frames, LANES)
+        wide_ref[pair + 1] = scaled + scaled * jnp.tanh(scaled)
+
+    lane = lax.broadcasted_iota(jnp.int32, (rows, LANES), 1)
+
+    def stack_window(wide_ref, act_ref, pair):
+        before, after = wide_ref[pair, :, LANES:], wide_ref[pair + 2, :, :LANES]
+        for tile, value in enumerate(
+            (before, wide_ref[pair + 1, :, :LANES], wide_ref[pair + 1, :, LANES:])
+        ):
+            spill = pltpu.roll(after, channels - tile * (LANES - channels), 1)
+            value = jnp.where(lane < channels, value, spill)
+            for shift in range(3):
+                moved = value
+                if shift:
+                    moved = jnp.where(frame_of_row >= shift, pltpu.roll(value, shift, 0), 0.0)
+                act_ref[
+                    2 - shift, pair, 1 : height + 1, :, tile * LANES : (tile + 1) * LANES
+                ] = moved.astype(jnp.bfloat16).reshape(height, frames, LANES)
 
     def both(row):
         vector = vector_ref[row : row + 1, :]
         return jnp.concatenate([vector, vector], axis=1)
 
-    def spread_weights(weight_ref):
-        big_ref[...] = jnp.zeros_like(big_ref)
-        for tap in range(9):
-            for side in range(2):
-                for step in range(3):
-                    first = (tap * 4 + side + step) * LANES
-                    big_ref[
-                        first : first + channels, side * LANES : side * LANES + channels
-                    ] = weight_ref[tap * 3 + step]
-
-    def convolve(first_pair, count):
-        parts = []
-        for tap in range(9):
-            step_t, step_h = tap // 3, tap % 3
-            for step in range(4):
-                parts.append(
-                    jnp.concatenate(
-                        [
-                            act_ref[
-                                step_t, 2 * (first_pair + i) + step, step_h : step_h + height
-                            ].reshape(rows, LANES)
-                            for i in range(count)
-                        ],
-                        axis=0,
-                    )
-                )
+    def convolve(act_ref, big_ref, first_pair, count):
+        parts = [
+            act_ref[
+                tap // 3, first_pair : first_pair + count, tap % 3 : tap % 3 + height
+            ].reshape(
+                count * rows, 3 * LANES
+            )
+            for tap in range(9)
+        ]
         stack = jnp.concatenate(parts, axis=1)
         return jnp.dot(stack, big_ref[...], preferred_element_type=jnp.float32)
 
-    act_ref[:, :, 0] = jnp.zeros_like(act_ref[:, :, 0])
-    act_ref[:, :, height + 1] = jnp.zeros_like(act_ref[:, :, height + 1])
-    act_ref[:, 0] = jnp.zeros_like(act_ref[:, 0])
+    for act_ref in (act_first_ref, act_second_ref):
+        act_ref[:, :, 0] = jnp.zeros_like(act_ref[:, :, 0])
+        act_ref[:, :, height + 1] = jnp.zeros_like(act_ref[:, :, height + 1])
+    wide_first_ref[0] = jnp.zeros_like(wide_first_ref[0])
+    wide_second_ref[pairs] = jnp.zeros_like(wide_second_ref[pairs])
+    block_ref[:, height] = jnp.zeros_like(block_ref[:, height])
 
     gain_first, gain_second = both(0), both(2)
     bias_first, bias_second = both(1), both(3)
 
-    spread_weights(weight_first_ref)
-
-    @pl.loop(0, pairs)
-    def _(pair):
-        values = jnp.concatenate(
-            [x_ref[2 * pair + side].reshape(rows, LANES) for side in range(2)], axis=1
-        )
-        activate(pair, values, gain_first)
-
-    group = 3
-
-    @pl.loop(0, (pairs - 1) // group)
-    def _(step):
-        result = convolve(step * group, group) + bias_first
-        for i in range(group):
-            conv_ref[step * group + i] = result[i * rows : (i + 1) * rows]
-
-    spread_weights(weight_second_ref)
-
-    @pl.loop(0, pairs - 1)
-    def _(pair):
-        activate(pair, conv_ref[pair], gain_second)
-
-    block_ref[:, height] = jnp.zeros_like(block_ref[:, height])
-    pair_count = 2
-
-    @pl.loop(0, (pairs - 2) // pair_count)
-    def _(step):
-        result = convolve(1 + step * pair_count, pair_count) + bias_second
-        for i in range(pair_count):
-            pair = 1 + step * pair_count + i
+    def first_window(acts, windows):
+        for pair in acts:
+            values = jnp.concatenate(
+                [x_ref[2 * pair + side].reshape(rows, LANES) for side in range(2)], axis=1
+            )
+            activate(wide_first_ref, pair, values, gain_first)
+        for pair in windows:
+            stack_window(wide_first_ref, act_first_ref, pair)
+
+    def second_window(acts, windows):
+        for pair in acts:
+            activate(wide_second_ref, pair, conv_ref[pair], gain_second)
+        for pair in windows:
+            stack_window(wide_second_ref, act_second_ref, pair)
+
+    def first_conv(todo):
+        result = convolve(act_first_ref, big_first_ref, todo[0], len(todo)) + bias_first
+        for i, pair in enumerate(todo):
+            conv_ref[pair] = result[i * rows : (i + 1) * rows]
+
+    def second_conv(todo):
+        result = convolve(act_second_ref, big_second_ref, todo[0], len(todo)) + bias_second
+        for i, pair in enumerate(todo):
             for side in range(2):
                 value = result[i * rows : (i + 1) * rows, side * LANES : (side + 1) * LANES]
                 value = value.reshape(height, frames, LANES) + x_ref[2 * pair + side]
@@ -387,35 +421,65 @@
                 value = jnp.where((column >= 0) & (column < plan.width), value, 0.0)
                 block_ref[2 * pair + side, 0:height] = value.astype(jnp.bfloat16)
 
-    big_reduce_ref[...] = jnp.zeros_like(big_reduce_ref)
-    for tap in range(9):
-        big_reduce_ref[tap * LANES : tap * LANES + channels, 0:channels] = weight_reduce_ref[tap]
+    outputs, half_rows = plan.own // 2, height // 2
+    size = half_rows * frames
+
+    def reduce_conv(todo):
+        stacks = [
+            jnp.concatenate(
+                [
+                    jnp.concatenate(
+                        [
+                            block_ref[LEFT + 2 * j + tap % 3, 2 * i + tap // 3]
+                            for i in range(half_rows)
+                        ],
+                        axis=0,
+                    )
+                    for tap in range(9)
+                ],
+                axis=1,
+            )
+            for j in todo
+        ]
+        result = jnp.dot(
+            jnp.concatenate(stacks, axis=0),
+            big_reduce_ref[...],
+            preferred_element_type=jnp.float32,
+        )
+        for i, j in enumerate(todo):
+            reduced_ref[j] = result[i * size : (i + 1) * size] + vector_ref[4:5, :]
+
+    last = pairs - 1
+    cuts = [0] + [last * (i + 1) // CHUNKS for i in range(CHUNKS)]
+    first_chunks = [range(a, b) for a, b in zip(cuts[:-1], cuts[1:])]
+    second_cuts = [1] + [cut - 1 for cut in cuts[1:-1]] + [last]
+    second_chunks = [range(a, b) for a, b in zip(second_cuts[:-1], second_cuts[1:])]
+    done = 0
+    reduced_until = 0
+    for step in range(CHUNKS + 4):
+        if 0 <= step - 1 < CHUNKS:
+            first_conv(first_chunks[step - 1])
+        if 0 <= step - 3 < CHUNKS and len(second_chunks[step - 3]):
+            second_conv(second_chunks[step - 3])
+        if 0 <= step - 4 < CHUNKS:
+            until = min(second_chunks[step - 4].stop - 2, outputs)
+            if until > reduced_until:
+                reduce_conv(range(reduced_until, until))
+                reduced_until = until
+        if step < CHUNKS:
+            until = first_chunks[step].stop + 1
+            first_window(range(done, until), first_chunks[step])
+            done = until
+        if 0 <= step - 2 < CHUNKS:
+            second_window(first_chunks[step - 2], second_chunks[step - 2])
 
     length = jnp.int32(0)
     for clip in range(lengths_ref.shape[0]):
         length = length + jnp.where(stored_ref[clip] == slot, lengths_ref[clip], 0)
 
-    outputs, half_rows = plan.own // 2, height // 2
-    columns = []
-    for j in range(outputs):
-        parts = []
-        for tap in range(9):
-            step_h, step_w = tap // 3, tap % 3
-            parts.append(
-                jnp.concatenate(
-                    [block_ref[LEFT + 2 * j + step_w, 2 * i + step_h] for i in range(half_rows)],
-                    axis=0,
-                )
-            )
-        stack = jnp.concatenate(parts, axis=1)
-        columns.append(stack)
-    stack = jnp.concatenate(columns, axis=0)
-    reduced = jnp.dot(stack, big_reduce_ref[...], preferred_element_type=jnp.float32)
-    reduced = reduced + vector_ref[4:5, :]
     alive = lax.broadcasted_iota(jnp.int32, (half_rows * frames, LANES), 0) % frames < length
-    size = half_rows * frames
     merged = merge_columns(
-        plan, [jnp.where(alive, reduced[j * size : (j + 1) * size], 0.0) for j in range(outputs)]
+        plan, [jnp.where(alive, reduced_ref[j], 0.0) for j in range(outputs)]
     )
     for tile, value in enumerate(merged):
         for i in range(half_rows):
@@ -444,25 +508,27 @@
         out_specs=vmem,
         scratch_shapes=[
             pltpu.VMEM((plan.window, plan.height, plan.all_frames, LANES), jnp.float32),
-            pltpu.VMEM((3, plan.window + 2, plan.height + 2, plan.all_frames, LANES), jnp.bfloat16),
+            pltpu.VMEM((3, pairs, plan.height + 2, plan.all_frames, 3 * LANES), jnp.bfloat16),
+            pltpu.VMEM((3, pairs, plan.height + 2, plan.all_frames, 3 * LANES), jnp.bfloat16),
+            pltpu.VMEM((pairs + 2, rows, 2 * LANES), jnp.float32),
+            pltpu.VMEM((pairs + 2, rows, 2 * LANES), jnp.float32),
             pltpu.VMEM((pairs, rows, 2 * LANES), jnp.float32),
             pltpu.VMEM((plan.window, plan.height + 1, plan.all_frames, LANES), jnp.bfloat16),
-            pltpu.VMEM((9 * 4 * LANES, 2 * LANES), jnp.bfloat16),
-            pltpu.VMEM((9 * LANES, LANES), jnp.bfloat16),
+            pltpu.VMEM((plan.own // 2, rows // 2, LANES), jnp.float32),
             pltpu.VMEM((8, LANES), jnp.float32),
         ],
-        compiler_params=pltpu.CompilerParams(vmem_limit_bytes=48 * 2**20),
+        compiler_params=pltpu.CompilerParams(vmem_limit_bytes=26 * 2**20),
     )(
         lengths,
         stored_slot,
         pieces,
         gain_first.reshape(1, channels),
-        conv_first.reshape(27, channels, channels),
+        conv_first,
         bias_first.reshape(1, channels),
         gain_second.reshape(1, channels),
-        conv_second.reshape(27, channels, channels),
+        conv_second,
         bias_second.reshape(1, channels),
-        reduce_conv_weight.reshape(9, channels, channels),
+        reduce_conv_weight,
         reduce_conv_bias.reshape(1, channels),
     )
 
@@ -482,6 +548,9 @@
         ],
         axis=0,
     )
+    conv_first, conv_second, reduce_conv_weight = spread_weights(
+        plan, conv_first, conv_second, reduce_conv_weight
+    )
     pieces = lax.all_to_all(pieces, ("tm", "rows"), 0, 0, tiled=True)
     out = encode_window(
         plan, pieces, lengths, stored_slot, gain_first, conv_first, bias_first, gain_second,

time: 70.4 us -> 62 us (0.88)
  Pallas kernels: 21.5 us -> 12.8 us
  local copies, waits for them, and re-layouts: 3.94 us -> 7.41 us
  waiting for transfers between devices: 29 us -> 25.7 us
    pallas_call x1, Pallas kernels: 21.5 us -> 12.1 us  [encode_window(): pl.pallas_call(functools.partial(encode_kernel, plan), out_shape=jax.Shap...]
    all_to_all x1, waiting for transfers between devices: 21.8 us -> 17.9 us  [window_local(): pieces = lax.all_to_all(pieces, ('tm', 'rows'), 0, 0, tiled=True)]
    unnamed x22 -> x26, local copies, waits for them, and re-layouts: 1.29 us -> 4.76 us
  transfers between devices with their start and end apart: 2 -> 2, of which waited for: 2 -> 2; matrix products, arithmetic and copies ran while one was open for 0% -> 0% of each run, Pallas kernels for 0% -> 1%
where the time goes in v1:
time: 62 us; the launch traced here: 61.6 us
  waiting for transfers between devices  25.7 us (41%)
  Pallas kernels  12.8 us (21%)
  starting transfers between devices  12 us (19%)
  local copies, waits for them, and re-layouts  7.41 us (12%)
  blocking collectives  2.04 us (3%)
  other arithmetic  1.2 us (2%)
    all_to_all x1, waiting for transfers between devices, window_local(): pieces = lax.all_to_all(pieces, ('tm', 'rows'), 0, 0, tiled=True)  17.9 us
    pallas_call x1, Pallas kernels, encode_window(): pl.pallas_call(functools.partial(encode_kernel, plan), out_shape=jax.Shap...  12.1 us
    all_to_all x1, starting transfers between devices, window_local(): pieces = lax.all_to_all(pieces, ('tm', 'rows'), 0, 0, tiled=True)  8.46 us
    all_to_all x1, waiting for transfers between devices, window_local(): out = lax.all_to_all(out, ('tm', 'rows'), 0, 0, tiled=True)  7.76 us
    unnamed x26, local copies, waits for them, and re-layouts  4.76 us
    all_to_all x1, starting transfers between devices, window_local(): out = lax.all_to_all(out, ('tm', 'rows'), 0, 0, tiled=True)  3.52 us
    all_gather x1, blocking collectives, window_local(): both = lax.all_gather(out, 'clip', axis=0, tiled=True)  2.04 us
    transpose x1, local copies, waits for them, and re-layouts, window_local(): dense = features.transpose(0, 2, 1, 3).reshape(clips, piece_rows, -1)  1.33 us
  transfers between devices with their start and end apart: 2, of which 2 were waited for; matrix products, arithmetic and copies ran while one was open for 0% of the time, Pallas kernels for 1%

profile of v1, /device:TPU:0, one launch (start us, length us, event | category | flops | bytes accessed | tf_op | source)
XLA Modules:
  0.0 61.6 jit_solution(3606823155255732639)
XLA Ops:
  0.0 1.3 %copy.20 = bf16[4,2,4,9984]{3,2,1,0:T(4,128)(2,1)S(1)} copy(bf16[4,2,4,9984]{3,1,2,0:T(2,128)(2,1)} %bitcast.30) | data formatting | bytes 1277952 | tf_op jit(solution)/shard_map/transpose | solution.py:542
  1.3 0.1 reshape.42
  1.5 0.2 pad_slice_fusion.1
  1.7 0.0 copy-start.2
  1.7 1.0 %pad_maximum_fusion = bf16[16,8,3072]{2,1,0:T(8,128)(2,1)} fusion(bf16[4,8,3072]{2,1,0:T(8,128)(2,1)S(1)} %get-tuple-element.12, bf16[4,8,3072]{2,1,0:T(8,128)(2,1)S(1)} %get-tuple-element.13, bf16[4,8,3072]{2,1,0:T(8,128)(2,1)S(1)} %get-tuple-element.14, bf16[4,8,3072]{2,1,0:T(8,128)(2,1)S(1)} %get-tuple-element.11), kind=kLoop, calls=%fused_computation.2 | loop fusion | flops 1179648 | bytes 1572864 | tf_op jit(solution)/shard_map/concatenate | solution.py:544
  2.7 0.0 copy-start.5
  2.7 0.0 copy-start.6
  2.7 0.0 copy-start.7
  2.7 0.0 copy-start.8
  2.7 0.0 copy-start.9
  2.7 0.0 copy-start.10
  2.7 0.0 copy-start.11
  2.7 8.5 %all-to-all-start = ((bf16[16,8,3072]{2,1,0:T(8,128)(2,1)}), bf16[16,8,3072]{2,1,0:T(8,128)(2,1)S(1)}, u32[]{:S(2)}, u32[]{:S(2)}) async-start(bf16[16,8,3072]{2,1,0:T(8,128)(2,1)} %pad_maximum_fusion), calls=%async_computation | async-start | bytes 1572864 | tf_op jit(solution)/shard_map/all_to_all | solution.py:554
  11.2 0.0 copy-done.2
  11.2 0.0 copy-start.3
  11.2 1.1 %copy-done.3 = bf16[3,3,3,96,96]{4,3,2,1,0:T(8,128)(2,1)S(1)} copy-done((bf16[3,3,3,96,96]{4,3,2,1,0:T(8,128)(2,1)S(1)}, bf16[3,3,3,96,96]{4,3,2,1,0:T(8,128)(2,1)}, u32[]{:S(2)}) %copy-start.3) | copy-done | bytes 497688
  12.3 0.0 copy-start.4
  12.3 0.9 %copy-done.4 = bf16[3,3,96,96]{3,2,1,0:T(8,128)(2,1)S(1)} copy-done((bf16[3,3,96,96]{3,2,1,0:T(8,128)(2,1)S(1)}, bf16[3,3,96,96]{3,2,1,0:T(8,128)(2,1)}, u32[]{:S(2)}) %copy-start.4) | copy-done | bytes 165912
  13.2 0.6 %shard_map.118 = (bf16[3456,256]{1,0:T(8,128)(2,1)S(1)}, bf16[3456,256]{1,0:T(8,128)(2,1)S(1)}, bf16[1152,128]{1,0:T(8,128)(2,1)S(1)}) custom-call(bf16[27,96,96]{2,1,0:T(8,128)(2,1)S(1)} %bitcast.21, bf16[27,96,96]{2,1,0:T(8,128)(2,1)S(1)} %bitcast.22, bf16[9,96,96]{2,1,0:T(8,128)(2,1)S(1)} %bitcast.23), custom_call_target="tpu_custom_call" | custom-call | bytes 6291456 | tf_op jit(solution)/shard_map/pallas_call | solution.py:260
  13.9 0.0 copy-start
  13.9 1.2 %copy-done = bf16[3456,256]{1,0:T(8,128)(2,1)} copy-done((bf16[3456,256]{1,0:T(8,128)(2,1)}, bf16[3456,256]{1,0:T(8,128)(2,1)S(1)}, u32[]{:S(2)}) %copy-start) | copy-done | bytes 1769496
  15.1 17.9 %all-to-all-done.pieces_ref = bf16[16,8,3072]{2,1,0:T(8,128)(2,1)S(1)} async-done(((bf16[16,8,3072]{2,1,0:T(8,128)(2,1)}), bf16[16,8,3072]{2,1,0:T(8,128)(2,1)S(1)}, u32[]{:S(2)}, u32[]{:S(2)}) %all-to-all-start) | async-done | bytes 786464 | tf_op jit(solution)/shard_map/all_to_all | solution.py:554
  33.1 0.0 copy-done.5
  33.1 0.0 copy-done.6
  33.1 0.0 copy-done.7
  33.1 0.0 copy-done.8
  33.1 0.0 copy-done.9
  33.1 0.0 copy-done.10
  33.1 0.0 copy-done.11
  33.1 0.0 copy-start.1
  33.1 1.5 %copy-done.1 = bf16[3456,256]{1,0:T(8,128)(2,1)S(1)} copy-done((bf16[3456,256]{1,0:T(8,128)(2,1)S(1)}, bf16[3456,256]{1,0:T(8,128)(2,1)}, u32[]{:S(2)}) %copy-start.1) | copy-done | bytes 1769496
  34.6 0.0 copy-start.12
  34.6 12.1 %shard_map.119 = bf16[16,4,1280]{2,1,0:T(4,128)(2,1)} custom-call(s32[8]{0:T(128)S(1)} %copy-done.6, s32[8]{0:T(128)S(1)} %copy-done.5, bf16[16,8,3072]{2,1,0:T(8,128)(2,1)S(1)} %all-to-all-done.pieces_ref, f32[1,96]{1,0:T(1,128)S(1)} %bitcast.24, bf16[3456,256]{1,0:T(8,128)(2,1)S(1)} %get-tuple-element.8.big_first_ref, f32[1,96]{1,0:T(1,128)S(1)} %bitcast.25, ...), custom_call_target="tpu_custom_call" | custom-call | tf_op jit(solution)/shard_map/pallas_call | solution.py:502
  46.7 3.5 %all-to-all-start.1 = ((bf16[16,4,1280]{2,1,0:T(4,128)(2,1)}), bf16[16,4,1280]{2,1,0:T(4,128)(2,1)S(1)}, u32[]{:S(2)}, u32[]{:S(2)}) async-start(bf16[16,4,1280]{2,1,0:T(4,128)(2,1)} %shard_map.119), calls=%async_computation.1 | async-start | bytes 327680 | tf_op jit(solution)/shard_map/all_to_all | solution.py:559
  50.3 0.0 copy-done.12
  50.3 0.2 select_reduce_fusion
  50.5 7.8 %all-to-all-done.1 = bf16[16,4,1280]{2,1,0:T(4,128)(2,1)S(1)} async-done(((bf16[16,4,1280]{2,1,0:T(4,128)(2,1)}), bf16[16,4,1280]{2,1,0:T(4,128)(2,1)S(1)}, u32[]{:S(2)}, u32[]{:S(2)}) %all-to-all-start.1) | async-done | bytes 163872 | tf_op jit(solution)/shard_map/all_to_all | solution.py:559
  58.2 0.1 copy.21
  58.3 0.2 reshape.52
  58.5 2.0 %all_gather.3 = bf16[8,4,1,4992]{3,1,2,0:T(4,128)(2,1)S(1)} all-gather(bf16[4,4,1,4992]{3,1,2,0:T(4,128)(2,1)S(1)} %reshape.52), channel_id=1, replica_groups=mesh['tm'=4,'rows'=4,'clip'=2] {'clip'}, dimensions={0}, use_global_device_ids=true | all-gather | bytes 479232 | tf_op jit(solution)/shard_map/all_gather | solution.py:563
  60.5 0.3 fusion
  60.8 0.7 %copy.23 = bf16[4,4,1,4992]{3,1,2,0:T(4,128)(2,1)} copy(bf16[4,4,1,4992]{3,0,1,2:T(4,128)(2,1)S(1)} %fusion) | data formatting | bytes 319488 | tf_op jit(solution)/shard_map/convert_element_type | solution.py:571
  (2 shorter events, 0.0 us)
Async XLA Ops:
  1.7 9.5 %copy-start.2 = (bf16[3,3,3,96,96]{4,3,2,1,0:T(8,128)(2,1)S(1)}, bf16[3,3,3,96,96]{4,3,2,1,0:T(8,128)(2,1)}, u32[]{:S(2)}) copy-start(bf16[3,3,3,96,96]{4,3,2,1,0:T(8,128)(2,1)} %param.17) | copy-start | bytes 1492996
  2.7 30.4 %copy-start.5 = (s32[8]{0:T(128)S(1)}, s32[8]{0:T(128)}, u32[]{:S(2)}) copy-start(s32[8]{0:T(128)} %stored_ref.1) | copy-start | bytes 100
  2.7 30.4 %copy-start.6 = (s32[8]{0:T(128)S(1)}, s32[8]{0:T(128)}, u32[]{:S(2)}) copy-start(s32[8]{0:T(128)} %lengths_ref.1) | copy-start | bytes 100
  2.7 30.4 %copy-start.7 = (f32[96]{0:T(128)S(1)}, f32[96]{0:T(128)}, u32[]{:S(2)}) copy-start(f32[96]{0:T(128)} %param.16) | copy-start | bytes 1156
  2.7 30.4 %copy-start.8 = (f32[96]{0:T(128)S(1)}, f32[96]{0:T(128)}, u32[]{:S(2)}) copy-start(f32[96]{0:T(128)} %param.18) | copy-start | bytes 1156
  2.7 30.4 %copy-start.9 = (f32[96]{0:T(128)S(1)}, f32[96]{0:T(128)}, u32[]{:S(2)}) copy-start(f32[96]{0:T(128)} %param.19) | copy-start | bytes 1156
  2.7 30.4 %copy-start.10 = (f32[96]{0:T(128)S(1)}, f32[96]{0:T(128)}, u32[]{:S(2)}) copy-start(f32[96]{0:T(128)} %param.21) | copy-start | bytes 1156
  2.7 30.4 %copy-start.11 = (f32[96]{0:T(128)S(1)}, f32[96]{0:T(128)}, u32[]{:S(2)}) copy-start(f32[96]{0:T(128)} %param.23) | copy-start | bytes 1156
  2.7 30.3 %all-to-all-start = ((bf16[16,8,3072]{2,1,0:T(8,128)(2,1)}), bf16[16,8,3072]{2,1,0:T(8,128)(2,1)S(1)}, u32[]{:S(2)}, u32[]{:S(2)}) async-start(bf16[16,8,3072]{2,1,0:T(8,128)(2,1)} %pad_maximum_fusion), calls=%async_computation | async-start | bytes 1572864 | tf_op jit(solution)/shard_map/all_to_all | solution.py:554
  11.2 1.1 %copy-start.3 = (bf16[3,3,3,96,96]{4,3,2,1,0:T(8,128)(2,1)S(1)}, bf16[3,3,3,96,96]{4,3,2,1,0:T(8,128)(2,1)}, u32[]{:S(2)}) copy-start(bf16[3,3,3,96,96]{4,3,2,1,0:T(8,128)(2,1)} %param.20) | copy-start | bytes 1492996
  12.3 0.9 %copy-start.4 = (bf16[3,3,96,96]{3,2,1,0:T(8,128)(2,1)S(1)}, bf16[3,3,96,96]{3,2,1,0:T(8,128)(2,1)}, u32[]{:S(2)}) copy-start(bf16[3,3,96,96]{3,2,1,0:T(8,128)(2,1)} %param.22) | copy-start | bytes 497668
  13.9 1.2 %copy-start = (bf16[3456,256]{1,0:T(8,128)(2,1)}, bf16[3456,256]{1,0:T(8,128)(2,1)S(1)}, u32[]{:S(2)}) copy-start(bf16[3456,256]{1,0:T(8,128)(2,1)S(1)} %get-tuple-element.9.big_second_ref) | copy-start | bytes 5308420
  33.1 1.5 %copy-start.1 = (bf16[3456,256]{1,0:T(8,128)(2,1)S(1)}, bf16[3456,256]{1,0:T(8,128)(2,1)}, u32[]{:S(2)}) copy-start(bf16[3456,256]{1,0:T(8,128)(2,1)} %copy-done) | copy-start | bytes 5308420
  34.6 15.7 %copy-start.12 = (s32[8]{0:T(128)S(1)}, s32[8]{0:T(128)}, u32[]{:S(2)}) copy-start(s32[8]{0:T(128)} %param.15) | copy-start | bytes 100
  46.7 11.5 %all-to-all-start.1 = ((bf16[16,4,1280]{2,1,0:T(4,128)(2,1)}), bf16[16,4,1280]{2,1,0:T(4,128)(2,1)S(1)}, u32[]{:S(2)}, u32[]{:S(2)}) async-start(bf16[16,4,1280]{2,1,0:T(4,128)(2,1)} %shard_map.119), calls=%async_computation.1 | async-start | bytes 327680 | tf_op jit(solution)/shard_map/all_to_all | solution.py:559

commit v2 on v1

--- a/solution.py
+++ b/solution.py
@@ -191,9 +191,11 @@
             and self.width % (2 * self.parts) == 0
             and 3 * (LANES - self.channels) == self.channels
             and self.band == 2
+            and self.cores == 2
             and self.band * self.frames == 8
             and self.all_frames == 16
             and (self.window * self.channels) % LANES == 0
+            and (self.width * self.channels) % LANES == 0
         )
 
 
@@ -228,47 +230,139 @@
     return merged
 
 
-def weights_kernel(plan, first_ref, second_ref, reduce_ref, big_first_ref, big_second_ref, big_reduce_ref):
+def pack_kernel(plan, source_ref, out_ref, features_ref, wide_ref, copy_sems):
+    channels, frames = plan.channels, plan.frames
+    copies = [
+        pltpu.make_async_copy(source_ref.at[clip], features_ref.at[clip], copy_sems.at[clip])
+        for clip in range(plan.clips)
+    ]
+    for copy in copies:
+        copy.start()
+    lead = -(-LEFT * channels // LANES) * LANES
+    inner = plan.width * channels
+    ahead, count = lead // LANES, inner // LANES
+    wide_ref[:, :ahead] = jnp.zeros((plan.clips, ahead, 8, LANES), jnp.float32)
+    after = wide_ref.shape[1] - ahead - count
+    wide_ref[:, ahead + count :] = jnp.zeros((plan.clips, after, 8, LANES), jnp.float32)
+    for clip in range(plan.clips):
+        copies[clip].wait()
+        for frame in range(frames):
+            rows = features_ref[clip, frame].astype(jnp.float32)
+            for tile in range(count):
+                wide_ref[clip, ahead + tile, pl.ds(frame, plan.band, stride=frames), :] = rows[
+                    :, tile * LANES : (tile + 1) * LANES
+                ]
+        for q in range(plan.parts):
+            start = lead + (q * plan.own - LEFT) * channels
+            off = start % LANES
+            for tile in range(plan.window * channels // LANES):
+                first = start // LANES + tile
+                value = wide_ref[clip, first]
+                if off:
+                    following = wide_ref[clip, first + 1]
+                    value = jnp.where(lanes_of(value.shape) >= off, value, following)
+                    value = pltpu.roll(value, LANES - off, 1)
+                out_ref[q * plan.clips + clip, :, tile * LANES : (tile + 1) * LANES] = (
+                    value.astype(jnp.bfloat16)
+                )
+
+
+def pack(plan, features):
+    channels = plan.channels
+    lead = -(-LEFT * channels // LANES) * LANES
+    total = -(-(lead + (plan.width + RIGHT) * channels) // LANES)
+    vmem = pl.BlockSpec(memory_space=pltpu.VMEM)
+    return pl.pallas_call(
+        functools.partial(pack_kernel, plan),
+        out_shape=jax.ShapeDtypeStruct(
+            (plan.devices, plan.band * plan.frames, plan.window * channels), jnp.bfloat16
+        ),
+        in_specs=[pl.BlockSpec(memory_space=pltpu.HBM)],
+        out_specs=vmem,
+        scratch_shapes=[
+            pltpu.VMEM(features.shape, features.dtype),
+            pltpu.VMEM((plan.clips, total, plan.band * plan.frames, LANES), jnp.float32),
+            pltpu.SemaphoreType.DMA((plan.clips,)),
+        ],
+        compiler_params=pltpu.CompilerParams(vmem_limit_bytes=16 * 2**20),
+    )(features)
+
+
+def finish_kernel(plan, stored_ref, owner_ref, mine_ref, other_ref, out_ref):
+    clips, channels = plan.clips, plan.channels
+    core = lax.axis_index("clip")
+    used = plan.own // 2 * channels
+    lane = lanes_of((plan.frames, LANES))
+    for place in range(clips):
+        source = jnp.int32(0)
+        for clip in range(stored_ref.shape[0]):
+            here = owner_ref[clip] == core * clips + place
+            source = source + jnp.where(here, stored_ref[clip], 0)
+        local = source % clips
+        is_mine = source // clips == core
+        tiles = [None] * (plan.parts * used // LANES)
+        for q in range(plan.parts):
+            piece = jnp.where(
+                is_mine, mine_ref[q * clips + local], other_ref[q * clips + local]
+            ).astype(jnp.float32)
+            first, off = q * used // LANES, q * used % LANES
+            before = tiles[first] if off else None
+            for index in range(piece.shape[1] // LANES):
+                value = piece[:, index * LANES : (index + 1) * LANES]
+                turned = pltpu.roll(value, off, 1) if off else value
+                if first + index < len(tiles):
+                    tiles[first + index] = jnp.where(lane >= off, turned, before) if off else turned
+                before = turned
+            if first + index + 1 < len(tiles):
+                tiles[first + index + 1] = turned
+        for index, value in enumerate(tiles):
+            out_ref[place, :, index * LANES : (index + 1) * LANES] = value.astype(jnp.bfloat16)
+
+
+def finish(plan, stored_slot, owner_slot, mine, other):
+    vmem = pl.BlockSpec(memory_space=pltpu.VMEM)
+    smem = pl.BlockSpec(memory_space=pltpu.SMEM)
+    width = plan.parts * (plan.own // 2) * plan.channels
+    return pl.pallas_call(
+        functools.partial(finish_kernel, plan),
+        out_shape=jax.ShapeDtypeStruct((plan.clips, plan.frames, width), jnp.bfloat16),
+        in_specs=[smem, smem, vmem, vmem],
+        out_specs=vmem,
+        compiler_params=pltpu.CompilerParams(vmem_limit_bytes=16 * 2**20),
+    )(stored_slot, owner_slot, mine, other)
+
+
+def weight_rows():
+    conv, reduction = 9 * 3 * LANES, 9 * LANES
+    return conv, 2 * conv, 2 * conv + reduction
+
+
+def spread_conv(plan, weight_ref, big_ref, base):
     channels = plan.channels
     spare = LANES - channels
-    for weight_ref, big_ref in ((first_ref, big_first_ref), (second_ref, big_second_ref)):
-        big_ref[...] = jnp.zeros_like(big_ref)
-        for tap in range(9):
-            for side in range(2):
-                for step in range(3):
-                    tile = side + step
-                    along = pl.ds(side * LANES, channels)
-                    if tile < 3:
-                        first = (tap * 3 + tile) * LANES
-                        big_ref[first : first + channels, along] = weight_ref[tap * 3 + step]
-                        continue
-                    for tile in range(3):
-                        first = (tap * 3 + tile) * LANES + channels
-                        big_ref[first : first + spare, along] = weight_ref[
-                            tap * 3 + step, tile * spare : (tile + 1) * spare
-                        ]
-    big_reduce_ref[...] = jnp.zeros_like(big_reduce_ref)
+    count = 9 * 3 * LANES
+    big_ref[base : base + count] = jnp.zeros((count, 2 * LANES), big_ref.dtype)
     for tap in range(9):
-        big_reduce_ref[tap * LANES : tap * LANES + channels, 0:channels] = reduce_ref[tap]
-
-
-def spread_weights(plan, conv_first, conv_second, reduce_conv_weight):
-    channels = plan.channels
-    vmem = pl.BlockSpec(memory_space=pltpu.VMEM)
-    conv = jax.ShapeDtypeStruct((9 * 3 * LANES, 2 * LANES), jnp.bfloat16)
-    reduction = jax.ShapeDtypeStruct((9 * LANES, LANES), jnp.bfloat16)
-    return pl.pallas_call(
-        functools.partial(weights_kernel, plan),
-        out_shape=(conv, conv, reduction),
-        in_specs=[vmem] * 3,
-        out_specs=(vmem,) * 3,
-        compiler_params=pltpu.CompilerParams(vmem_limit_bytes=16 * 2**20),
-        cost_estimate=pl.CostEstimate(flops=0, transcendentals=0, bytes_accessed=6 * 2**20),
-    )(
-        conv_first.reshape(27, channels, channels),
-        conv_second.reshape(27, channels, channels),
-        reduce_conv_weight.reshape(9, channels, channels),
-    )
+        for side in range(2):
+            for step in range(3):
+                tile = side + step
+                along = pl.ds(side * LANES, channels)
+                if tile < 3:
+                    first = base + (tap * 3 + tile) * LANES
+                    big_ref[first : first + channels, along] = weight_ref[tap * 3 + step]
+                    continue
+                for tile in range(3):
+                    first = base + (tap * 3 + tile) * LANES + channels
+                    big_ref[first : first + spare, along] = weight_ref[
+                        tap * 3 + step, tile * spare : (tile + 1) * spare
+                    ]
+
+
+def spread_reduction(plan, weight_ref, big_ref, base):
+    big_ref[base:] = jnp.zeros_like(big_ref[base:])
+    for tap in range(9):
+        first = base + tap * LANES
+        big_ref[first : first + plan.channels, 0 : plan.channels] = weight_ref[tap]
 
 
 def encode_kernel(
@@ -276,13 +370,13 @@
     lengths_ref,
     stored_ref,
     pieces_ref,
+    conv_first_ref,
+    conv_second_ref,
+    conv_reduce_ref,
     gain_first_ref,
-    big_first_ref,
     bias_first_ref,
     gain_second_ref,
-    big_second_ref,
     bias_second_ref,
-    big_reduce_ref,
     bias_reduce_ref,
     out_ref,
     x_ref,
@@ -294,11 +388,17 @@
     block_ref,
     reduced_ref,
     vector_ref,
+    weights_ref,
 ):
     frames, height, pairs, channels = plan.all_frames, plan.height, plan.pairs, plan.channels
     rows = height * frames
     part = lax.axis_index("tm")
     slot = lax.axis_index("clip") * plan.clips + lax.axis_index("rows")
+
+    conv_rows, reduce_rows, end_rows = weight_rows()
+    spread_conv(plan, conv_first_ref, weights_ref, 0)
+    spread_conv(plan, conv_second_ref, weights_ref, conv_rows)
+    spread_reduction(plan, conv_reduce_ref, weights_ref, reduce_rows)
 
     vector_ref[...] = jnp.zeros_like(vector_ref)
     for row, ref in enumerate(
@@ -369,7 +469,10 @@
         vector = vector_ref[row : row + 1, :]
         return jnp.concatenate([vector, vector], axis=1)
 
-    def convolve(act_ref, big_ref, first_pair, count):
+    first_weights = slice(0, conv_rows)
+    second_weights = slice(conv_rows, reduce_rows)
+
+    def convolve(act_ref, weights, first_pair, count):
         parts = [
             act_ref[
                 tap // 3, first_pair : first_pair + count, tap % 3 : tap % 3 + height
@@ -379,7 +482,7 @@
             for tap in range(9)
         ]
         stack = jnp.concatenate(parts, axis=1)
-        return jnp.dot(stack, big_ref[...], preferred_element_type=jnp.float32)
+        return jnp.dot(stack, weights_ref[weights], preferred_element_type=jnp.float32)
 
     for act_ref in (act_first_ref, act_second_ref):
         act_ref[:, :, 0] = jnp.zeros_like(act_ref[:, :, 0])
@@ -407,12 +510,12 @@
             stack_window(wide_second_ref, act_second_ref, pair)
 
     def first_conv(todo):
-        result = convolve(act_first_ref, big_first_ref, todo[0], len(todo)) + bias_first
+        result = convolve(act_first_ref, first_weights, todo[0], len(todo)) + bias_first
         for i, pair in enumerate(todo):
             conv_ref[pair] = result[i * rows : (i + 1) * rows]
 
     def second_conv(todo):
-        result = convolve(act_second_ref, big_second_ref, todo[0], len(todo)) + bias_second
+        result = convolve(act_second_ref, second_weights, todo[0], len(todo)) + bias_second
         for i, pair in enumerate(todo):
             for side in range(2):
                 value = result[i * rows : (i + 1) * rows, side * LANES : (side + 1) * LANES]
@@ -443,7 +546,7 @@
         ]
         result = jnp.dot(
             jnp.concatenate(stacks, axis=0),
-            big_reduce_ref[...],
+            weights_ref[reduce_rows:end_rows, 0:LANES],
             preferred_element_type=jnp.float32,
         )
         for i, j in enumerate(todo):
@@ -516,19 +619,20 @@
             pltpu.VMEM((plan.window, plan.height + 1, plan.all_frames, LANES), jnp.bfloat16),
             pltpu.VMEM((plan.own // 2, rows // 2, LANES), jnp.float32),
             pltpu.VMEM((8, LANES), jnp.float32),
+            pltpu.VMEM((weight_rows()[2], 2 * LANES), jnp.bfloat16),
         ],
-        compiler_params=pltpu.CompilerParams(vmem_limit_bytes=26 * 2**20),
+        compiler_params=pltpu.CompilerParams(vmem_limit_bytes=32 * 2**20),
     )(
         lengths,
         stored_slot,
         pieces,
+        conv_first.reshape(27, channels, channels),
+        conv_second.reshape(27, channels, channels),
+        reduce_conv_weight.reshape(9, channels, channels),
         gain_first.reshape(1, channels),
-        conv_first,
         bias_first.reshape(1, channels),
         gain_second.reshape(1, channels),
-        conv_second,
         bias_second.reshape(1, channels),
-        reduce_conv_weight,
         reduce_conv_bias.reshape(1, channels),
     )
 
@@ -537,38 +641,18 @@
     plan, features, lengths, stored_slot, owner_slot, gain_first, conv_first, bias_first,
     gain_second, conv_second, bias_second, reduce_conv_weight, reduce_conv_bias,
 ):
-    channels, clips, parts = plan.channels, plan.clips, plan.parts
-    piece_rows = plan.frames * plan.band
-    dense = features.transpose(0, 2, 1, 3).reshape(clips, piece_rows, -1)
-    dense = jnp.pad(dense, ((0, 0), (0, 0), (LEFT * channels, RIGHT * channels)))
-    pieces = jnp.concatenate(
-        [
-            dense[:, :, q * plan.own * channels :][:, :, : plan.window * channels]
-            for q in range(parts)
-        ],
-        axis=0,
-    )
-    conv_first, conv_second, reduce_conv_weight = spread_weights(
-        plan, conv_first, conv_second, reduce_conv_weight
-    )
+    clips = plan.clips
+    pieces = pack(plan, features)
     pieces = lax.all_to_all(pieces, ("tm", "rows"), 0, 0, tiled=True)
     out = encode_window(
         plan, pieces, lengths, stored_slot, gain_first, conv_first, bias_first, gain_second,
         conv_second, bias_second, reduce_conv_weight, reduce_conv_bias,
     )
     out = lax.all_to_all(out, ("tm", "rows"), 0, 0, tiled=True)
-    used = plan.own // 2 * channels
-    out = out[:, :, :used].reshape(parts, clips, plan.frames, used)
-    out = out.transpose(1, 2, 0, 3).reshape(clips, plan.frames, 1, parts * used)
-    both = lax.all_gather(out, "clip", axis=0, tiled=True)
-    numbers = jnp.arange(stored_slot.shape[0], dtype=jnp.int32)
-    my_slots = lax.axis_index("clip") * clips + numbers[:clips]
-    wanted = (owner_slot[None, :] == my_slots[:, None]).astype(jnp.int32)
-    source = jnp.sum(wanted * stored_slot[None, :], axis=1)
-    weights = (source[:, None] == numbers[None, :]).astype(out.dtype)
-    return jnp.einsum(
-        "ki,iabc->kabc", weights, both, preferred_element_type=jnp.float32
-    ).astype(out.dtype)
+    swap = [(core, plan.cores - 1 - core) for core in range(plan.cores)]
+    other = lax.ppermute(out, "clip", swap)
+    out = finish(plan, stored_slot, owner_slot, out, other)
+    return out.reshape(clips, plan.frames, 1, out.shape[2])
 
 
 def solution(mesh):

time: 62 us -> 59.1 us (0.953)
  blocking collectives: 2.04 us -> 40.7 us
  waiting for transfers between devices: 25.7 us -> 1.39 us
  starting transfers between devices: 12 us -> 0.01 us
  local copies, waits for them, and re-layouts: 7.41 us -> 1.75 us
  Pallas kernels: 12.8 us -> 14.9 us
  other arithmetic: 1.2 us -> 0 us
    all_to_all x0 -> x2, blocking collectives: none -> 40.7 us  [the longest x1 30.1 us: window_local(): pieces = lax.all_to_all(pieces, ('tm', 'rows'), 0, 0, tiled=True)]
    all_to_all x2 -> x0, waiting for transfers between devices: 25.7 us -> none  [the longest x1 17.9 us: window_local(): pieces = lax.all_to_all(pieces, ('tm', 'rows'), 0, 0, tiled=True)]
    all_to_all x2 -> x0, starting transfers between devices: 12 us -> none  [the longest x1 8.46 us: window_local(): pieces = lax.all_to_all(pieces, ('tm', 'rows'), 0, 0, tiled=True)]
    unnamed x26 -> x24, local copies, waits for them, and re-layouts: 4.76 us -> 1.75 us
    pallas_call x1 -> x2, Pallas kernels: 0.64 us -> 2.98 us  [the longest x1 1.61 us: pack(): pl.pallas_call(functools.partial(pack_kernel, plan), out_shape=jax.ShapeD...]
    all_gather x1 -> x0, blocking collectives: 2.04 us -> none  [window_local(): both = lax.all_gather(out, 'clip', axis=0, tiled=True)]
    transpose x2 -> x0, local copies, waits for them, and re-layouts: 1.41 us -> none  [the longest x1 1.33 us: window_local(): dense = features.transpose(0, 2, 1, 3).reshape(clips, piece_rows, -1)]
    ppermute x0 -> x1, waiting for transfers between devices: none -> 1.39 us  [window_local(): other = lax.ppermute(out, 'clip', swap)]
  transfers between devices with their start and end apart: 2 -> 1, of which waited for: 2 -> 1; matrix products, arithmetic and copies ran while one was open for 0% -> 0% of each run, Pallas kernels for 1% -> 0%
where the time goes in v2:
time: 59.1 us; the launch traced here: 58.9 us
  blocking collectives  40.7 us (69%)
  Pallas kernels  14.9 us (25%)
  local copies, waits for them, and re-layouts  1.75 us (3%)
  waiting for transfers between devices  1.39 us (2%)
    all_to_all x1, blocking collectives, window_local(): pieces = lax.all_to_all(pieces, ('tm', 'rows'), 0, 0, tiled=True)  30.1 us
    pallas_call x1, Pallas kernels, encode_window(): pl.pallas_call(functools.partial(encode_kernel, plan), out_shape=jax.Shap...  11.9 us
    all_to_all x1, blocking collectives, window_local(): out = lax.all_to_all(out, ('tm', 'rows'), 0, 0, tiled=True)  10.7 us
    unnamed x24, local copies, waits for them, and re-layouts  1.75 us
    pallas_call x1, Pallas kernels, pack(): pl.pallas_call(functools.partial(pack_kernel, plan), out_shape=jax.ShapeD...  1.61 us
    ppermute x1, waiting for transfers between devices, window_local(): other = lax.ppermute(out, 'clip', swap)  1.39 us
    pallas_call x1, Pallas kernels, finish(): pl.pallas_call(functools.partial(finish_kernel, plan), out_shape=jax.Shap...  1.38 us
  transfers between devices with their start and end apart: 1, of which 1 were waited for; matrix products, arithmetic and copies ran while one was open for 0% of the time, Pallas kernels for 0%

profile of v2, /device:TPU:0, one launch (start us, length us, event | category | flops | bytes accessed | tf_op | source)
XLA Modules:
  0.0 58.9 jit_solution(3372183738827620141)
XLA Ops:
  0.0 0.0 copy-start.2
  0.0 1.1 %copy-done.2 = bf16[4,4,2,9984]{3,2,1,0:T(2,128)(2,1)S(1)} copy-done((bf16[4,4,2,9984]{3,2,1,0:T(2,128)(2,1)S(1)}, bf16[4,4,2,9984]{3,2,1,0:T(2,128)(2,1)}, u32[]{:S(2)}) %copy-start.2) | copy-done | bytes 639000
  1.1 1.6 %shard_map.118 = bf16[16,8,3072]{2,1,0:T(8,128)(2,1)S(1)} custom-call(bf16[4,4,2,9984]{3,2,1,0:T(2,128)(2,1)S(1)} %copy-done.2), custom_call_target="tpu_custom_call" | custom-call | tf_op jit(solution)/shard_map/pallas_call | solution.py:275
  2.7 0.0 copy-start
  2.7 0.0 copy-start.1
  2.7 0.0 copy-start.3
  2.7 0.0 copy-start.7
  2.7 0.0 copy-start.8
  2.8 0.0 copy-start.9
  2.8 0.0 copy-start.10
  2.8 30.1 %all_to_all.10.pieces_ref = bf16[16,8,3072]{2,1,0:T(8,128)(2,1)S(1)} all-to-all(bf16[16,8,3072]{2,1,0:T(8,128)(2,1)S(1)} %shard_map.118), channel_id=1, replica_groups=mesh['tm'=4,'rows'=4,'clip'=2] {'tm','rows'}, dimensions={0} | all-to-all | bytes 1572864 | tf_op jit(solution)/shard_map/all_to_all | solution.py:646
  32.8 0.0 copy-start.4
  32.8 0.0 copy-start.5
  32.8 0.0 copy-start.6
  32.8 0.0 copy-done
  32.8 0.0 copy-done.1
  32.9 0.0 copy-done.3
  32.9 0.0 copy-done.7
  32.9 0.0 copy-done.8
  32.9 0.0 copy-done.9
  32.9 0.0 copy-done.10
  32.9 0.6 copy-done.4
  33.5 0.0 copy-done.5
  33.5 0.0 copy-done.6
  33.5 11.9 %shard_map.119 = bf16[16,4,1280]{2,1,0:T(4,128)(2,1)S(1)} custom-call(s32[8]{0:T(128)S(1)} %copy-done.5, s32[8]{0:T(128)S(1)} %copy-done.4, bf16[16,8,3072]{2,1,0:T(8,128)(2,1)S(1)} %all_to_all.10.pieces_ref, bf16[27,96,96]{2,1,0:T(8,128)(2,1)S(1)} %bitcast.11, bf16[27,96,96]{2,1,0:T(8,128)(2,1)S(1)} %bitcast.12, bf16[9,96,96]{2,1,0:T(8,128)(2,1)S(1)} %bitcast.13, ...), custom_call_target="tpu_custom_call" | custom-call | tf_op jit(solution)/shard_map/pallas_call | solution.py:605
  45.4 0.0 copy-start.11
  45.4 10.7 %all_to_all.11.mine_ref = bf16[16,4,1280]{2,1,0:T(4,128)(2,1)S(1)} all-to-all(bf16[16,4,1280]{2,1,0:T(4,128)(2,1)S(1)} %shard_map.119), channel_id=1, replica_groups=mesh['tm'=4,'rows'=4,'clip'=2] {'tm','rows'}, dimensions={0} | all-to-all | bytes 327680 | tf_op jit(solution)/shard_map/all_to_all | solution.py:651
  56.1 0.0 collective-permute-start
  56.1 1.4 %collective-permute-done.other_ref = bf16[16,4,1280]{2,1,0:T(4,128)(2,1)S(1)} collective-permute-done((bf16[16,4,1280]{2,1,0:T(4,128)(2,1)S(1)}, bf16[16,4,1280]{2,1,0:T(4,128)(2,1)S(1)}, u32[]{:S(2)}, u32[]{:S(2)}) %collective-permute-start) | collective-permute-done | bytes 163872 | tf_op jit(solution)/shard_map/ppermute | solution.py:653
  57.5 0.0 copy-done.11
  57.5 1.4 %shard_map.120 = bf16[4,4,4992]{2,1,0:T(4,128)(2,1)} custom-call(s32[8]{0:T(128)S(1)} %copy-done.4, s32[8]{0:T(128)S(1)} %copy-done.11, bf16[16,4,1280]{2,1,0:T(4,128)(2,1)S(1)} %all_to_all.11.mine_ref, bf16[16,4,1280]{2,1,0:T(4,128)(2,1)S(1)} %collective-permute-done.other_ref), custom_call_target="tpu_custom_call" | custom-call | tf_op jit(solution)/shard_map/pallas_call | solution.py:326
Async XLA Ops:
  0.0 1.1 %copy-start.2 = (bf16[4,4,2,9984]{3,2,1,0:T(2,128)(2,1)S(1)}, bf16[4,4,2,9984]{3,2,1,0:T(2,128)(2,1)}, u32[]{:S(2)}) copy-start(bf16[4,4,2,9984]{3,2,1,0:T(2,128)(2,1)} %source_ref.1) | copy-start | bytes 1916932
  2.7 30.1 %copy-start = (bf16[3,3,3,96,96]{4,3,2,1,0:T(8,128)(2,1)S(1)}, bf16[3,3,3,96,96]{4,3,2,1,0:T(8,128)(2,1)}, u32[]{:S(2)}) copy-start(bf16[3,3,3,96,96]{4,3,2,1,0:T(8,128)(2,1)} %param.17) | copy-start | bytes 1492996
  2.7 30.1 %copy-start.1 = (bf16[3,3,3,96,96]{4,3,2,1,0:T(8,128)(2,1)S(1)}, bf16[3,3,3,96,96]{4,3,2,1,0:T(8,128)(2,1)}, u32[]{:S(2)}) copy-start(bf16[3,3,3,96,96]{4,3,2,1,0:T(8,128)(2,1)} %param.20) | copy-start | bytes 1492996
  2.7 30.1 %copy-start.3 = (bf16[3,3,96,96]{3,2,1,0:T(8,128)(2,1)S(1)}, bf16[3,3,96,96]{3,2,1,0:T(8,128)(2,1)}, u32[]{:S(2)}) copy-start(bf16[3,3,96,96]{3,2,1,0:T(8,128)(2,1)} %param.22) | copy-start | bytes 497668
  2.7 30.1 %copy-start.7 = (f32[96]{0:T(128)S(1)}, f32[96]{0:T(128)}, u32[]{:S(2)}) copy-start(f32[96]{0:T(128)} %param.18) | copy-start | bytes 1156
  2.7 30.1 %copy-start.8 = (f32[96]{0:T(128)S(1)}, f32[96]{0:T(128)}, u32[]{:S(2)}) copy-start(f32[96]{0:T(128)} %param.19) | copy-start | bytes 1156
  2.8 30.1 %copy-start.9 = (f32[96]{0:T(128)S(1)}, f32[96]{0:T(128)}, u32[]{:S(2)}) copy-start(f32[96]{0:T(128)} %param.21) | copy-start | bytes 1156
  2.8 30.1 %copy-start.10 = (f32[96]{0:T(128)S(1)}, f32[96]{0:T(128)}, u32[]{:S(2)}) copy-start(f32[96]{0:T(128)} %param.23) | copy-start | bytes 1156
  32.8 0.7 %copy-start.4 = (s32[8]{0:T(128)S(1)}, s32[8]{0:T(128)}, u32[]{:S(2)}) copy-start(s32[8]{0:T(128)} %stored_ref.3) | copy-start | bytes 100
  32.8 0.7 %copy-start.5 = (s32[8]{0:T(128)S(1)}, s32[8]{0:T(128)}, u32[]{:S(2)}) copy-start(s32[8]{0:T(128)} %lengths_ref.1) | copy-start | bytes 100
  32.8 0.7 %copy-start.6 = (f32[96]{0:T(128)S(1)}, f32[96]{0:T(128)}, u32[]{:S(2)}) copy-start(f32[96]{0:T(128)} %param.16) | copy-start | bytes 1156
  45.4 12.1 %copy-start.11 = (s32[8]{0:T(128)S(1)}, s32[8]{0:T(128)}, u32[]{:S(2)}) copy-start(s32[8]{0:T(128)} %owner_ref.1) | copy-start | bytes 100
  56.1 1.4 %collective-permute-start = (bf16[16,4,1280]{2,1,0:T(4,128)(2,1)S(1)}, bf16[16,4,1280]{2,1,0:T(4,128)(2,1)S(1)}, u32[]{:S(2)}, u32[]{:S(2)}) collective-permute-start(bf16[16,4,1280]{2,1,0:T(4,128)(2,1)S(1)} %all_to_all.11.mine_ref), channel_id=1, source_target_pairs={{0,1},{1,0},{2,3},{3,2},{4,5},{5,4},{6,7},{7,6},{8,9},{9,8},{10,11... | collective-permute-start | bytes 491528 | tf_op jit(solution)/shard_map/ppermute | solution.py:653

commit v3 on v2

--- a/solution.py
+++ b/solution.py
@@ -167,7 +167,8 @@
     ).astype(shard_piece.dtype)
 
 
-CHUNKS = 4
+CUTS = (4, 8, 12, 15)
+CHUNKS = len(CUTS)
 
 
 class Plan:
@@ -230,14 +231,49 @@
     return merged
 
 
-def pack_kernel(plan, source_ref, out_ref, features_ref, wide_ref, copy_sems):
+def slot_source(plan, stored_ref, owner_ref, place):
+    wanted = lax.axis_index("clip") * plan.clips + place
+    source = jnp.int32(0)
+    for clip in range(stored_ref.shape[0]):
+        source = source + jnp.where(owner_ref[clip] == wanted, stored_ref[clip], 0)
+    return source
+
+
+def vectors_kernel(
+    plan, lengths_ref, stored_ref, owner_ref, gain_first_ref, bias_first_ref, gain_second_ref,
+    bias_second_ref, bias_reduce_ref, vector_ref,
+):
+    vector_ref[...] = jnp.zeros_like(vector_ref)
+    for row, ref in enumerate(
+        (gain_first_ref, bias_first_ref, gain_second_ref, bias_second_ref, bias_reduce_ref)
+    ):
+        vector_ref[row : row + 1, 0 : plan.channels] = ref[...]
+    wanted = lax.axis_index("clip") * plan.clips + lax.axis_index("rows")
+    length = jnp.int32(0)
+    for clip in range(lengths_ref.shape[0]):
+        length = length + jnp.where(owner_ref[clip] == wanted, lengths_ref[clip], 0)
+    vector_ref[5:6, :] = jnp.full((1, LANES), length, jnp.int32).astype(jnp.float32)
+
+
+def gather_vectors(plan, lengths, stored_slot, owner_slot, vectors):
+    vmem = pl.BlockSpec(memory_space=pltpu.VMEM)
+    smem = pl.BlockSpec(memory_space=pltpu.SMEM)
+    return pl.pallas_call(
+        functools.partial(vectors_kernel, plan),
+        out_shape=jax.ShapeDtypeStruct((8, LANES), jnp.float32),
+        in_specs=[smem] * 3 + [vmem] * 5,
+        out_specs=vmem,
+        compiler_params=pltpu.CompilerParams(vmem_limit_bytes=4 * 2**20),
+    )(
+        lengths,
+        stored_slot,
+        owner_slot,
+        *(vector.reshape(1, plan.channels) for vector in vectors),
+    )
+
+
+def pack_kernel(plan, stored_ref, owner_ref, vector_ref, mine_ref, other_ref, out_ref, wide_ref):
     channels, frames = plan.channels, plan.frames
-    copies = [
-        pltpu.make_async_copy(source_ref.at[clip], features_ref.at[clip], copy_sems.at[clip])
-        for clip in range(plan.clips)
-    ]
-    for copy in copies:
-        copy.start()
     lead = -(-LEFT * channels // LANES) * LANES
     inner = plan.width * channels
     ahead, count = lead // LANES, inner // LANES
@@ -245,13 +281,26 @@
     after = wide_ref.shape[1] - ahead - count
     wide_ref[:, ahead + count :] = jnp.zeros((plan.clips, after, 8, LANES), jnp.float32)
     for clip in range(plan.clips):
-        copies[clip].wait()
-        for frame in range(frames):
-            rows = features_ref[clip, frame].astype(jnp.float32)
-            for tile in range(count):
-                wide_ref[clip, ahead + tile, pl.ds(frame, plan.band, stride=frames), :] = rows[
-                    :, tile * LANES : (tile + 1) * LANES
-                ]
+        source = slot_source(plan, stored_ref, owner_ref, clip)
+        local = source % plan.clips
+        is_mine = source // plan.clips == lax.axis_index("clip")
+
+        def spread_frames(features_ref):
+            for frame in range(frames):
+                rows = features_ref[local, frame].astype(jnp.float32)
+                for tile in range(count):
+                    wide_ref[clip, ahead + tile, pl.ds(frame, plan.band, stride=frames), :] = rows[
+                        :, tile * LANES : (tile + 1) * LANES
+                    ]
+
+        @pl.when(is_mine)
+        def _():
+            spread_frames(mine_ref)
+
+        @pl.when(jnp.logical_not(is_mine))
+        def _():
+            spread_frames(other_ref)
+
         for q in range(plan.parts):
             start = lead + (q * plan.own - LEFT) * channels
             off = start % LANES
@@ -262,49 +311,38 @@
                     following = wide_ref[clip, first + 1]
                     value = jnp.where(lanes_of(value.shape) >= off, value, following)
                     value = pltpu.roll(value, LANES - off, 1)
-                out_ref[q * plan.clips + clip, :, tile * LANES : (tile + 1) * LANES] = (
+                out_ref[clip * plan.parts + q, :, tile * LANES : (tile + 1) * LANES] = (
                     value.astype(jnp.bfloat16)
                 )
 
 
-def pack(plan, features):
+def pack(plan, stored_slot, owner_slot, vectors, mine, other):
     channels = plan.channels
     lead = -(-LEFT * channels // LANES) * LANES
     total = -(-(lead + (plan.width + RIGHT) * channels) // LANES)
     vmem = pl.BlockSpec(memory_space=pltpu.VMEM)
+    smem = pl.BlockSpec(memory_space=pltpu.SMEM)
+    piece_rows = plan.band * plan.frames
     return pl.pallas_call(
         functools.partial(pack_kernel, plan),
         out_shape=jax.ShapeDtypeStruct(
-            (plan.devices, plan.band * plan.frames, plan.window * channels), jnp.bfloat16
+            (plan.devices, piece_rows, plan.window * channels), jnp.bfloat16
         ),
-        in_specs=[pl.BlockSpec(memory_space=pltpu.HBM)],
+        in_specs=[smem, smem, pl.BlockSpec(memory_space=pl.ANY), vmem, vmem],
         out_specs=vmem,
-        scratch_shapes=[
-            pltpu.VMEM(features.shape, features.dtype),
-            pltpu.VMEM((plan.clips, total, plan.band * plan.frames, LANES), jnp.float32),
-            pltpu.SemaphoreType.DMA((plan.clips,)),
-        ],
+        scratch_shapes=[pltpu.VMEM((plan.clips, total, piece_rows, LANES), jnp.float32)],
         compiler_params=pltpu.CompilerParams(vmem_limit_bytes=16 * 2**20),
-    )(features)
-
-
-def finish_kernel(plan, stored_ref, owner_ref, mine_ref, other_ref, out_ref):
+    )(stored_slot, owner_slot, vectors, mine, other)
+
+
+def finish_kernel(plan, pieces_ref, out_ref):
     clips, channels = plan.clips, plan.channels
-    core = lax.axis_index("clip")
     used = plan.own // 2 * channels
     lane = lanes_of((plan.frames, LANES))
     for place in range(clips):
-        source = jnp.int32(0)
-        for clip in range(stored_ref.shape[0]):
-            here = owner_ref[clip] == core * clips + place
-            source = source + jnp.where(here, stored_ref[clip], 0)
-        local = source % clips
-        is_mine = source // clips == core
         tiles = [None] * (plan.parts * used // LANES)
         for q in range(plan.parts):
-            piece = jnp.where(
-                is_mine, mine_ref[q * clips + local], other_ref[q * clips + local]
-            ).astype(jnp.float32)
+            piece = pieces_ref[place * plan.parts + q].astype(jnp.float32)
             first, off = q * used // LANES, q * used % LANES
             before = tiles[first] if off else None
             for index in range(piece.shape[1] // LANES):
@@ -319,17 +357,16 @@
             out_ref[place, :, index * LANES : (index + 1) * LANES] = value.astype(jnp.bfloat16)
 
 
-def finish(plan, stored_slot, owner_slot, mine, other):
+def finish(plan, pieces):
     vmem = pl.BlockSpec(memory_space=pltpu.VMEM)
-    smem = pl.BlockSpec(memory_space=pltpu.SMEM)
     width = plan.parts * (plan.own // 2) * plan.channels
     return pl.pallas_call(
         functools.partial(finish_kernel, plan),
         out_shape=jax.ShapeDtypeStruct((plan.clips, plan.frames, width), jnp.bfloat16),
-        in_specs=[smem, smem, vmem, vmem],
+        in_specs=[vmem],
         out_specs=vmem,
         compiler_params=pltpu.CompilerParams(vmem_limit_bytes=16 * 2**20),
-    )(stored_slot, owner_slot, mine, other)
+    )(pieces)
 
 
 def weight_rows():
@@ -367,17 +404,11 @@
 
 def encode_kernel(
     plan,
-    lengths_ref,
-    stored_ref,
     pieces_ref,
+    vector_ref,
     conv_first_ref,
     conv_second_ref,
     conv_reduce_ref,
-    gain_first_ref,
-    bias_first_ref,
-    gain_second_ref,
-    bias_second_ref,
-    bias_reduce_ref,
     out_ref,
     x_ref,
     act_first_ref,
@@ -387,30 +418,22 @@
     conv_ref,
     block_ref,
     reduced_ref,
-    vector_ref,
     weights_ref,
 ):
     frames, height, pairs, channels = plan.all_frames, plan.height, plan.pairs, plan.channels
     rows = height * frames
     part = lax.axis_index("tm")
-    slot = lax.axis_index("clip") * plan.clips + lax.axis_index("rows")
 
     conv_rows, reduce_rows, end_rows = weight_rows()
     spread_conv(plan, conv_first_ref, weights_ref, 0)
     spread_conv(plan, conv_second_ref, weights_ref, conv_rows)
     spread_reduction(plan, conv_reduce_ref, weights_ref, reduce_rows)
 
-    vector_ref[...] = jnp.zeros_like(vector_ref)
-    for row, ref in enumerate(
-        (gain_first_ref, bias_first_ref, gain_second_ref, bias_second_ref, bias_reduce_ref)
-    ):
-        vector_ref[row : row + 1, 0:channels] = ref[...]
-
     half = plan.frames
     sublane = lax.broadcasted_iota(jnp.int32, (8, LANES), 0)
     for band in range(plan.bands):
         dense = [
-            pieces_ref[block * plan.bands + band].astype(jnp.float32)
+            pieces_ref[band * plan.blocks + block].astype(jnp.float32)
             for block in range(plan.blocks)
         ]
         for column in range(plan.window):
@@ -553,7 +576,7 @@
             reduced_ref[j] = result[i * size : (i + 1) * size] + vector_ref[4:5, :]
 
     last = pairs - 1
-    cuts = [0] + [last * (i + 1) // CHUNKS for i in range(CHUNKS)]
+    cuts = [0] + [last * end // CUTS[-1] for end in CUTS]
     first_chunks = [range(a, b) for a, b in zip(cuts[:-1], cuts[1:])]
     second_cuts = [1] + [cut - 1 for cut in cuts[1:-1]] + [last]
     second_chunks = [range(a, b) for a, b in zip(second_cuts[:-1], second_cuts[1:])]
@@ -576,11 +599,8 @@
         if 0 <= step - 2 < CHUNKS:
             second_window(first_chunks[step - 2], second_chunks[step - 2])
 
-    length = jnp.int32(0)
-    for clip in range(lengths_ref.shape[0]):
-        length = length + jnp.where(stored_ref[clip] == slot, lengths_ref[clip], 0)
-
-    alive = lax.broadcasted_iota(jnp.int32, (half_rows * frames, LANES), 0) % frames < length
+    alive = lax.broadcasted_iota(jnp.int32, (size, LANES), 0) % frames
+    alive = alive.astype(jnp.float32) < vector_ref[5:6, :]
     merged = merge_columns(
         plan, [jnp.where(alive, reduced_ref[j], 0.0) for j in range(outputs)]
     )
@@ -588,52 +608,43 @@
         for i in range(half_rows):
             for block in range(plan.blocks):
                 first = i * frames + block * plan.frames
-                out_ref[block * plan.bands + i, :, tile * LANES : (tile + 1) * LANES] = value[
+                out_ref[i * plan.blocks + block, :, tile * LANES : (tile + 1) * LANES] = value[
                     first : first + plan.frames
                 ].astype(jnp.bfloat16)
 
 
-def encode_window(
-    plan, pieces, lengths, stored_slot, gain_first, conv_first, bias_first, gain_second,
-    conv_second, bias_second, reduce_conv_weight, reduce_conv_bias,
-):
+def encode_window(plan, pieces, vectors, conv_first, conv_second, reduce_conv_weight):
     channels, pairs = plan.channels, plan.pairs
     rows = plan.height * plan.all_frames
     out_tiles = -(-plan.own // 2 * channels // LANES)
     vmem = pl.BlockSpec(memory_space=pltpu.VMEM)
-    smem = pl.BlockSpec(memory_space=pltpu.SMEM)
+    acts = pltpu.VMEM((3, pairs, plan.height + 2, plan.all_frames, 3 * LANES), jnp.bfloat16)
+    wide = pltpu.VMEM((pairs + 2, rows, 2 * LANES), jnp.float32)
     return pl.pallas_call(
         functools.partial(encode_kernel, plan),
         out_shape=jax.ShapeDtypeStruct(
             (plan.devices, plan.frames, out_tiles * LANES), jnp.bfloat16
         ),
-        in_specs=[smem, smem] + [vmem] * 9,
+        in_specs=[vmem] * 5,
         out_specs=vmem,
         scratch_shapes=[
             pltpu.VMEM((plan.window, plan.height, plan.all_frames, LANES), jnp.float32),
-            pltpu.VMEM((3, pairs, plan.height + 2, plan.all_frames, 3 * LANES), jnp.bfloat16),
-            pltpu.VMEM((3, pairs, plan.height + 2, plan.all_frames, 3 * LANES), jnp.bfloat16),
-            pltpu.VMEM((pairs + 2, rows, 2 * LANES), jnp.float32),
-            pltpu.VMEM((pairs + 2, rows, 2 * LANES), jnp.float32),
+            acts,
+            acts,
+            wide,
+            wide,
             pltpu.VMEM((pairs, rows, 2 * LANES), jnp.float32),
             pltpu.VMEM((plan.window, plan.height + 1, plan.all_frames, LANES), jnp.bfloat16),
             pltpu.VMEM((plan.own // 2, rows // 2, LANES), jnp.float32),
-            pltpu.VMEM((8, LANES), jnp.float32),
             pltpu.VMEM((weight_rows()[2], 2 * LANES), jnp.bfloat16),
         ],
         compiler_params=pltpu.CompilerParams(vmem_limit_bytes=32 * 2**20),
     )(
-        lengths,
-        stored_slot,
         pieces,
+        vectors,
         conv_first.reshape(27, channels, channels),
         conv_second.reshape(27, channels, channels),
         reduce_conv_weight.reshape(9, channels, channels),
-        gain_first.reshape(1, channels),
-        bias_first.reshape(1, channels),
-        gain_second.reshape(1, channels),
-        bias_second.reshape(1, channels),
-        reduce_conv_bias.reshape(1, channels),
     )
 
 
@@ -641,18 +652,16 @@
     plan, features, lengths, stored_slot, owner_slot, gain_first, conv_first, bias_first,
     gain_second, conv_second, bias_second, reduce_conv_weight, reduce_conv_bias,
 ):
-    clips = plan.clips
-    pieces = pack(plan, features)
-    pieces = lax.all_to_all(pieces, ("tm", "rows"), 0, 0, tiled=True)
-    out = encode_window(
-        plan, pieces, lengths, stored_slot, gain_first, conv_first, bias_first, gain_second,
-        conv_second, bias_second, reduce_conv_weight, reduce_conv_bias,
-    )
-    out = lax.all_to_all(out, ("tm", "rows"), 0, 0, tiled=True)
     swap = [(core, plan.cores - 1 - core) for core in range(plan.cores)]
-    other = lax.ppermute(out, "clip", swap)
-    out = finish(plan, stored_slot, owner_slot, out, other)
-    return out.reshape(clips, plan.frames, 1, out.shape[2])
+    other = lax.ppermute(features, "clip", swap)
+    vectors = (gain_first, bias_first, gain_second, bias_second, reduce_conv_bias)
+    vectors = gather_vectors(plan, lengths, stored_slot, owner_slot, vectors)
+    pieces = pack(plan, stored_slot, owner_slot, vectors, features, other)
+    pieces = lax.all_to_all(pieces, ("rows", "tm"), 0, 0, tiled=True)
+    out = encode_window(plan, pieces, vectors, conv_first, conv_second, reduce_conv_weight)
+    out = lax.all_to_all(out, ("rows", "tm"), 0, 0, tiled=True)
+    out = finish(plan, out)
+    return out.reshape(plan.clips, plan.frames, 1, out.shape[2])
 
 
 def solution(mesh):

time: 59.1 us -> 58.4 us (0.988)
  waiting for transfers between devices: 1.39 us -> 0.57 us
    ppermute x1, waiting for transfers between devices: 1.39 us -> 0.57 us  [window_local(): other = lax.ppermute(features, 'clip', swap)]
  transfers between devices with their start and end apart: 1 -> 1, of which waited for: 1 -> 1; matrix products, arithmetic and copies ran while one was open for 0% -> 0% of each run, Pallas kernels for 0% -> 1%
where the time goes in v3:
time: 58.4 us; the launch traced here: 58.2 us
  blocking collectives  40.8 us (70%)
  Pallas kernels  14.4 us (25%)
  local copies, waits for them, and re-layouts  1.83 us (3%)
    all_to_all x1, blocking collectives, window_local(): pieces = lax.all_to_all(pieces, ('rows', 'tm'), 0, 0, tiled=True)  29.7 us
    pallas_call x1, Pallas kernels, encode_window(): pl.pallas_call(functools.partial(encode_kernel, plan), out_shape=jax.Shap...  11.6 us
    all_to_all x1, blocking collectives, window_local(): out = lax.all_to_all(out, ('rows', 'tm'), 0, 0, tiled=True)  11.1 us
    unnamed x24, local copies, waits for them, and re-layouts  1.83 us
    pallas_call x1, Pallas kernels, pack(): pl.pallas_call(functools.partial(pack_kernel, plan), out_shape=jax.ShapeD...  1.39 us
  transfers between devices with their start and end apart: 1, of which 1 were waited for; matrix products, arithmetic and copies ran while one was open for 0% of the time, Pallas kernels for 1%

profile of v3, /device:TPU:0, one launch (start us, length us, event | category | flops | bytes accessed | tf_op | source)
XLA Modules:
  0.0 58.2 jit_solution(18095930634284896152)
XLA Ops:
  0.0 0.5 collective-permute-start
  0.5 0.0 copy-start.11
  0.5 0.0 copy-start.7
  0.5 0.0 copy-start.8
  0.5 0.0 copy-start.9
  0.5 0.0 copy-start.10
  0.5 0.0 copy-start.4
  0.5 0.0 copy-start.5
  0.5 0.0 copy-start.6
  0.5 0.6 %copy-done.11 = f32[96]{0:T(128)S(1)} copy-done((f32[96]{0:T(128)S(1)}, f32[96]{0:T(128)}, u32[]{:S(2)}) %copy-start.11) | copy-done | bytes 408
  1.1 0.0 copy-done.7
  1.1 0.0 copy-done.8
  1.1 0.0 copy-done.9
  1.2 0.0 copy-done.10
  1.2 0.0 copy-done.4
  1.2 0.0 copy-done.5
  1.2 0.0 copy-done.6
  1.2 0.6 shard_map.118.vector_ref
  1.8 0.6 collective-permute-done.other_ref
  2.4 0.0 copy-start.2
  2.4 1.1 %copy-done.2 = bf16[4,4,2,9984]{3,2,1,0:T(2,128)(2,1)S(1)} copy-done((bf16[4,4,2,9984]{3,2,1,0:T(2,128)(2,1)S(1)}, bf16[4,4,2,9984]{3,2,1,0:T(2,128)(2,1)}, u32[]{:S(2)}) %copy-start.2) | copy-done | bytes 639000
  3.4 1.4 %shard_map.119 = bf16[16,8,3072]{2,1,0:T(8,128)(2,1)S(1)} custom-call(s32[8]{0:T(128)S(1)} %copy-done.4, s32[8]{0:T(128)S(1)} %copy-done.5, f32[8,128]{1,0:T(8,128)S(1)} %shard_map.118.vector_ref, bf16[4,4,2,9984]{3,2,1,0:T(2,128)(2,1)S(1)} %copy-done.2, bf16[4,4,2,9984]{3,2,1,0:T(2,128)(2,1)S(1)} %collective-permute-done.other_ref), custom_call_target="tpu_custom_call" | custom-call | tf_op jit(solution)/shard_map/pallas_call | solution.py:326
  4.8 0.0 copy-start
  4.9 0.0 copy-start.1
  4.9 0.0 copy-start.3
  4.9 29.7 %all_to_all.10.pieces_ref = bf16[16,8,3072]{2,1,0:T(8,128)(2,1)S(1)} all-to-all(bf16[16,8,3072]{2,1,0:T(8,128)(2,1)S(1)} %shard_map.119), channel_id=1, replica_groups=mesh['tm'=4,'rows'=4,'clip'=2] {'rows','tm'}, dimensions={0} | all-to-all | bytes 1572864 | tf_op jit(solution)/shard_map/all_to_all | solution.py:660
  34.6 0.0 copy-done
  34.6 0.0 copy-done.1
  34.6 0.0 copy-done.3
  34.6 11.6 %shard_map.120 = bf16[16,4,1280]{2,1,0:T(4,128)(2,1)S(1)} custom-call(bf16[16,8,3072]{2,1,0:T(8,128)(2,1)S(1)} %all_to_all.10.pieces_ref, f32[8,128]{1,0:T(8,128)S(1)} %shard_map.118.vector_ref, bf16[27,96,96]{2,1,0:T(8,128)(2,1)S(1)} %bitcast.11, bf16[27,96,96]{2,1,0:T(8,128)(2,1)S(1)} %bitcast.12, bf16[9,96,96]{2,1,0:T(8,128)(2,1)S(1)} %bitcast.13), custom_call_target="tpu_custom_call" | custom-call | tf_op jit(solution)/shard_map/pallas_call | solution.py:623
  46.3 11.1 %all_to_all.11.pieces_ref = bf16[16,4,1280]{2,1,0:T(4,128)(2,1)S(1)} all-to-all(bf16[16,4,1280]{2,1,0:T(4,128)(2,1)S(1)} %shard_map.120), channel_id=1, replica_groups=mesh['tm'=4,'rows'=4,'clip'=2] {'rows','tm'}, dimensions={0} | all-to-all | bytes 327680 | tf_op jit(solution)/shard_map/all_to_all | solution.py:662
  57.4 0.8 %shard_map.121 = bf16[4,4,4992]{2,1,0:T(4,128)(2,1)} custom-call(bf16[16,4,1280]{2,1,0:T(4,128)(2,1)S(1)} %all_to_all.11.pieces_ref), custom_call_target="tpu_custom_call" | custom-call | tf_op jit(solution)/shard_map/pallas_call | solution.py:363
Async XLA Ops:
  0.0 2.4 %collective-permute-start = (bf16[4,4,2,9984]{3,2,1,0:T(2,128)(2,1)}, bf16[4,4,2,9984]{3,2,1,0:T(2,128)(2,1)S(1)}, u32[]{:S(2)}, u32[]{:S(2)}) collective-permute-start(bf16[4,4,2,9984]{3,2,1,0:T(2,128)(2,1)} %mine_ref.1), channel_id=1, source_target_pairs={{0,1},{1,0},{2,3},{3,2},{4,5},{5,4},{6,7},{7,6},{8,9},{9,8},{10,11... | collective-permute-start | bytes 1916936 | tf_op jit(solution)/shard_map/ppermute | solution.py:656
  0.5 0.7 %copy-start.11 = (f32[96]{0:T(128)S(1)}, f32[96]{0:T(128)}, u32[]{:S(2)}) copy-start(f32[96]{0:T(128)} %param.23) | copy-start | bytes 1156
  0.5 0.7 %copy-start.7 = (f32[96]{0:T(128)S(1)}, f32[96]{0:T(128)}, u32[]{:S(2)}) copy-start(f32[96]{0:T(128)} %param.16) | copy-start | bytes 1156
  0.5 0.7 %copy-start.8 = (f32[96]{0:T(128)S(1)}, f32[96]{0:T(128)}, u32[]{:S(2)}) copy-start(f32[96]{0:T(128)} %param.18) | copy-start | bytes 1156
  0.5 0.7 %copy-start.9 = (f32[96]{0:T(128)S(1)}, f32[96]{0:T(128)}, u32[]{:S(2)}) copy-start(f32[96]{0:T(128)} %param.19) | copy-start | bytes 1156
  0.5 0.7 %copy-start.10 = (f32[96]{0:T(128)S(1)}, f32[96]{0:T(128)}, u32[]{:S(2)}) copy-start(f32[96]{0:T(128)} %param.21) | copy-start | bytes 1156
  0.5 0.7 %copy-start.4 = (s32[8]{0:T(128)S(1)}, s32[8]{0:T(128)}, u32[]{:S(2)}) copy-start(s32[8]{0:T(128)} %stored_ref.3) | copy-start | bytes 100
  0.5 0.7 %copy-start.5 = (s32[8]{0:T(128)S(1)}, s32[8]{0:T(128)}, u32[]{:S(2)}) copy-start(s32[8]{0:T(128)} %owner_ref.3) | copy-start | bytes 100
  0.5 0.7 %copy-start.6 = (s32[8]{0:T(128)S(1)}, s32[8]{0:T(128)}, u32[]{:S(2)}) copy-start(s32[8]{0:T(128)} %lengths_ref.1) | copy-start | bytes 100
  2.4 1.1 %copy-start.2 = (bf16[4,4,2,9984]{3,2,1,0:T(2,128)(2,1)S(1)}, bf16[4,4,2,9984]{3,2,1,0:T(2,128)(2,1)}, u32[]{:S(2)}) copy-start(bf16[4,4,2,9984]{3,2,1,0:T(2,128)(2,1)} %mine_ref.1) | copy-start | bytes 1916932
  4.8 29.8 %copy-start = (bf16[3,3,3,96,96]{4,3,2,1,0:T(8,128)(2,1)S(1)}, bf16[3,3,3,96,96]{4,3,2,1,0:T(8,128)(2,1)}, u32[]{:S(2)}) copy-start(bf16[3,3,3,96,96]{4,3,2,1,0:T(8,128)(2,1)} %param.17) | copy-start | bytes 1492996
  4.9 29.8 %copy-start.1 = (bf16[3,3,3,96,96]{4,3,2,1,0:T(8,128)(2,1)S(1)}, bf16[3,3,3,96,96]{4,3,2,1,0:T(8,128)(2,1)}, u32[]{:S(2)}) copy-start(bf16[3,3,3,96,96]{4,3,2,1,0:T(8,128)(2,1)} %param.20) | copy-start | bytes 1492996
  4.9 29.8 %copy-start.3 = (bf16[3,3,96,96]{3,2,1,0:T(8,128)(2,1)S(1)}, bf16[3,3,96,96]{3,2,1,0:T(8,128)(2,1)}, u32[]{:S(2)}) copy-start(bf16[3,3,96,96]{3,2,1,0:T(8,128)(2,1)} %param.22) | copy-start | bytes 497668

commit v4 on v3

--- a/solution.py
+++ b/solution.py
@@ -167,7 +167,7 @@
     ).astype(shard_piece.dtype)
 
 
-CUTS = (4, 8, 12, 15)
+CUTS = (3, 7, 11, 15)
 CHUNKS = len(CUTS)
 
 
@@ -270,6 +270,23 @@
         owner_slot,
         *(vector.reshape(1, plan.channels) for vector in vectors),
     )
+
+
+def stage_kernel(source_ref, out_ref, sem):
+    copy = pltpu.make_async_copy(source_ref, out_ref, sem)
+    copy.start()
+    copy.wait()
+
+
+def stage(features):
+    return pl.pallas_call(
+        stage_kernel,
+        out_shape=jax.ShapeDtypeStruct(features.shape, features.dtype),
+        in_specs=[pl.BlockSpec(memory_space=pl.ANY)],
+        out_specs=pl.BlockSpec(memory_space=pltpu.VMEM),
+        scratch_shapes=[pltpu.SemaphoreType.DMA],
+        compiler_params=pltpu.CompilerParams(vmem_limit_bytes=4 * 2**20),
+    )(features)
 
 
 def pack_kernel(plan, stored_ref, owner_ref, vector_ref, mine_ref, other_ref, out_ref, wide_ref):
@@ -654,9 +671,10 @@
 ):
     swap = [(core, plan.cores - 1 - core) for core in range(plan.cores)]
     other = lax.ppermute(features, "clip", swap)
+    mine = stage(features)
     vectors = (gain_first, bias_first, gain_second, bias_second, reduce_conv_bias)
     vectors = gather_vectors(plan, lengths, stored_slot, owner_slot, vectors)
-    pieces = pack(plan, stored_slot, owner_slot, vectors, features, other)
+    pieces = pack(plan, stored_slot, owner_slot, vectors, mine, other)
     pieces = lax.all_to_all(pieces, ("rows", "tm"), 0, 0, tiled=True)
     out = encode_window(plan, pieces, vectors, conv_first, conv_second, reduce_conv_weight)
     out = lax.all_to_all(out, ("rows", "tm"), 0, 0, tiled=True)

time: 58.4 us -> 57.7 us (0.988)
  transfers between devices with their start and end apart: 1 -> 1, of which waited for: 1 -> 0; matrix products, arithmetic and copies ran while one was open for 0% -> 0% of each run, Pallas kernels for 1% -> 1%
where the time goes in v4:
time: 57.7 us; the launch traced here: 57.4 us
  blocking collectives  40.8 us (71%)
  Pallas kernels  14.2 us (25%)
  local copies, waits for them, and re-layouts  1.77 us (3%)
    all_to_all x1, blocking collectives, window_local(): pieces = lax.all_to_all(pieces, ('rows', 'tm'), 0, 0, tiled=True)  29.7 us
    pallas_call x1, Pallas kernels, encode_window(): pl.pallas_call(functools.partial(encode_kernel, plan), out_shape=jax.Shap...  11.3 us
    all_to_all x1, blocking collectives, window_local(): out = lax.all_to_all(out, ('rows', 'tm'), 0, 0, tiled=True)  11.1 us
    unnamed x24, local copies, waits for them, and re-layouts  1.77 us
    pallas_call x1, Pallas kernels, pack(): pl.pallas_call(functools.partial(pack_kernel, plan), out_shape=jax.ShapeD...  1.4 us
  transfers between devices with their start and end apart: 1, of which 0 were waited for; matrix products, arithmetic and copies ran while one was open for 0% of the time, Pallas kernels for 1%

profile of v4, /device:TPU:0, one launch (start us, length us, event | category | flops | bytes accessed | tf_op | source)
XLA Modules:
  0.0 57.4 jit_solution(14608634224509681675)
XLA Ops:
  0.0 0.5 collective-permute-start
  0.5 0.0 copy-start.2
  0.5 1.1 %copy-done.2 = bf16[4,4,2,9984]{3,2,1,0:T(2,128)(2,1)S(1)} copy-done((bf16[4,4,2,9984]{3,2,1,0:T(2,128)(2,1)S(1)}, bf16[4,4,2,9984]{3,2,1,0:T(2,128)(2,1)}, u32[]{:S(2)}) %copy-start.2) | copy-done | bytes 639000
  1.5 0.0 copy-start.7
  1.5 0.0 copy-start.8
  1.5 0.0 copy-start.9
  1.5 0.0 copy-start.10
  1.5 0.0 copy-start.11
  1.6 0.2 shard_map.119.mine_ref
  1.8 0.0 copy-start.4
  1.8 0.0 copy-start.5
  1.8 0.0 copy-start.6
  1.8 0.4 copy-done.7
  2.2 0.0 copy-done.8
  2.2 0.0 copy-done.9
  2.2 0.0 copy-done.10
  2.2 0.0 copy-done.11
  2.3 0.2 copy-done.4
  2.4 0.0 copy-done.5
  2.4 0.0 copy-done.6
  2.5 0.6 shard_map.118.vector_ref
  3.0 0.0 collective-permute-done.other_ref
  3.0 1.4 %shard_map.120 = bf16[16,8,3072]{2,1,0:T(8,128)(2,1)S(1)} custom-call(s32[8]{0:T(128)S(1)} %copy-done.4, s32[8]{0:T(128)S(1)} %copy-done.5, f32[8,128]{1,0:T(8,128)S(1)} %shard_map.118.vector_ref, bf16[4,4,2,9984]{3,2,1,0:T(2,128)(2,1)S(1)} %shard_map.119.mine_ref, bf16[4,4,2,9984]{3,2,1,0:T(2,128)(2,1)S(1)} %collective-permute-done.other_ref), custom_call_target="tpu_custom_call" | custom-call | tf_op jit(solution)/shard_map/pallas_call | solution.py:343
  4.4 0.0 copy-start
  4.5 0.0 copy-start.1
  4.5 0.0 copy-start.3
  4.5 29.7 %all_to_all.10.pieces_ref = bf16[16,8,3072]{2,1,0:T(8,128)(2,1)S(1)} all-to-all(bf16[16,8,3072]{2,1,0:T(8,128)(2,1)S(1)} %shard_map.120), channel_id=1, replica_groups=mesh['tm'=4,'rows'=4,'clip'=2] {'rows','tm'}, dimensions={0} | all-to-all | bytes 1572864 | tf_op jit(solution)/shard_map/all_to_all | solution.py:678
  34.2 0.0 copy-done
  34.2 0.0 copy-done.1
  34.2 0.0 copy-done.3
  34.2 11.3 %shard_map.121 = bf16[16,4,1280]{2,1,0:T(4,128)(2,1)S(1)} custom-call(bf16[16,8,3072]{2,1,0:T(8,128)(2,1)S(1)} %all_to_all.10.pieces_ref, f32[8,128]{1,0:T(8,128)S(1)} %shard_map.118.vector_ref, bf16[27,96,96]{2,1,0:T(8,128)(2,1)S(1)} %bitcast.11, bf16[27,96,96]{2,1,0:T(8,128)(2,1)S(1)} %bitcast.12, bf16[9,96,96]{2,1,0:T(8,128)(2,1)S(1)} %bitcast.13), custom_call_target="tpu_custom_call" | custom-call | tf_op jit(solution)/shard_map/pallas_call | solution.py:640
  45.5 11.1 %all_to_all.11.pieces_ref = bf16[16,4,1280]{2,1,0:T(4,128)(2,1)S(1)} all-to-all(bf16[16,4,1280]{2,1,0:T(4,128)(2,1)S(1)} %shard_map.121), channel_id=1, replica_groups=mesh['tm'=4,'rows'=4,'clip'=2] {'rows','tm'}, dimensions={0} | all-to-all | bytes 327680 | tf_op jit(solution)/shard_map/all_to_all | solution.py:680
  56.6 0.8 %shard_map.122 = bf16[4,4,4992]{2,1,0:T(4,128)(2,1)} custom-call(bf16[16,4,1280]{2,1,0:T(4,128)(2,1)S(1)} %all_to_all.11.pieces_ref), custom_call_target="tpu_custom_call" | custom-call | tf_op jit(solution)/shard_map/pallas_call | solution.py:380
Async XLA Ops:
  0.0 3.0 %collective-permute-start = (bf16[4,4,2,9984]{3,2,1,0:T(2,128)(2,1)}, bf16[4,4,2,9984]{3,2,1,0:T(2,128)(2,1)S(1)}, u32[]{:S(2)}, u32[]{:S(2)}) collective-permute-start(bf16[4,4,2,9984]{3,2,1,0:T(2,128)(2,1)} %source_ref.1), channel_id=1, source_target_pairs={{0,1},{1,0},{2,3},{3,2},{4,5},{5,4},{6,7},{7,6},{8,9},{9,8},{10,11... | collective-permute-start | bytes 1916936 | tf_op jit(solution)/shard_map/ppermute | solution.py:673
  0.5 1.1 %copy-start.2 = (bf16[4,4,2,9984]{3,2,1,0:T(2,128)(2,1)S(1)}, bf16[4,4,2,9984]{3,2,1,0:T(2,128)(2,1)}, u32[]{:S(2)}) copy-start(bf16[4,4,2,9984]{3,2,1,0:T(2,128)(2,1)} %source_ref.1) | copy-start | bytes 1916932
  1.5 0.7 %copy-start.7 = (f32[96]{0:T(128)S(1)}, f32[96]{0:T(128)}, u32[]{:S(2)}) copy-start(f32[96]{0:T(128)} %param.16) | copy-start | bytes 1156
  1.5 0.7 %copy-start.8 = (f32[96]{0:T(128)S(1)}, f32[96]{0:T(128)}, u32[]{:S(2)}) copy-start(f32[96]{0:T(128)} %param.18) | copy-start | bytes 1156
  1.5 0.7 %copy-start.9 = (f32[96]{0:T(128)S(1)}, f32[96]{0:T(128)}, u32[]{:S(2)}) copy-start(f32[96]{0:T(128)} %param.19) | copy-start | bytes 1156
  1.5 0.7 %copy-start.10 = (f32[96]{0:T(128)S(1)}, f32[96]{0:T(128)}, u32[]{:S(2)}) copy-start(f32[96]{0:T(128)} %param.21) | copy-start | bytes 1156
  1.5 0.7 %copy-start.11 = (f32[96]{0:T(128)S(1)}, f32[96]{0:T(128)}, u32[]{:S(2)}) copy-start(f32[96]{0:T(128)} %param.23) | copy-start | bytes 1156
  1.8 0.7 %copy-start.4 = (s32[8]{0:T(128)S(1)}, s32[8]{0:T(128)}, u32[]{:S(2)}) copy-start(s32[8]{0:T(128)} %stored_ref.3) | copy-start | bytes 100
  1.8 0.7 %copy-start.5 = (s32[8]{0:T(128)S(1)}, s32[8]{0:T(128)}, u32[]{:S(2)}) copy-start(s32[8]{0:T(128)} %owner_ref.3) | copy-start | bytes 100
  1.8 0.7 %copy-start.6 = (s32[8]{0:T(128)S(1)}, s32[8]{0:T(128)}, u32[]{:S(2)}) copy-start(s32[8]{0:T(128)} %lengths_ref.1) | copy-start | bytes 100
  4.4 29.8 %copy-start = (bf16[3,3,3,96,96]{4,3,2,1,0:T(8,128)(2,1)S(1)}, bf16[3,3,3,96,96]{4,3,2,1,0:T(8,128)(2,1)}, u32[]{:S(2)}) copy-start(bf16[3,3,3,96,96]{4,3,2,1,0:T(8,128)(2,1)} %param.17) | copy-start | bytes 1492996
  4.5 29.8 %copy-start.1 = (bf16[3,3,3,96,96]{4,3,2,1,0:T(8,128)(2,1)S(1)}, bf16[3,3,3,96,96]{4,3,2,1,0:T(8,128)(2,1)}, u32[]{:S(2)}) copy-start(bf16[3,3,3,96,96]{4,3,2,1,0:T(8,128)(2,1)} %param.20) | copy-start | bytes 1492996
  4.5 29.8 %copy-start.3 = (bf16[3,3,96,96]{3,2,1,0:T(8,128)(2,1)S(1)}, bf16[3,3,96,96]{3,2,1,0:T(8,128)(2,1)}, u32[]{:S(2)}) copy-start(bf16[3,3,96,96]{3,2,1,0:T(8,128)(2,1)} %param.22) | copy-start | bytes 497668

commit v5 on v4

--- a/solution.py
+++ b/solution.py
@@ -474,7 +474,7 @@
         return jnp.where(across == along, 1.0, 0.0).astype(jnp.bfloat16)
 
     ones = sum_matrix()
-    frame_of_row = lax.broadcasted_iota(jnp.int32, (rows, LANES), 0) % frames
+    row_in_tile = lax.broadcasted_iota(jnp.int32, (height, frames // 8, 8, LANES), 2)
 
     def in_image(pair):
         lane = lax.broadcasted_iota(jnp.int32, (1, 2 * LANES), 1)
@@ -497,10 +497,15 @@
         ):
             spill = pltpu.roll(after, channels - tile * (LANES - channels), 1)
             value = jnp.where(lane < channels, value, spill)
+            value = value.reshape(height, frames // 8, 8, LANES)
             for shift in range(3):
                 moved = value
                 if shift:
-                    moved = jnp.where(frame_of_row >= shift, pltpu.roll(value, shift, 0), 0.0)
+                    turned = pltpu.roll(value, shift, 2)
+                    ahead = jnp.concatenate(
+                        [jnp.zeros_like(turned[:, :1]), turned[:, :-1]], axis=1
+                    )
+                    moved = jnp.where(row_in_tile >= shift, turned, ahead)
                 act_ref[
                     2 - shift, pair, 1 : height + 1, :, tile * LANES : (tile + 1) * LANES
                 ] = moved.astype(jnp.bfloat16).reshape(height, frames, LANES)

time: 57.7 us -> 57.3 us (level)
  no operation moved by 1% of the time
where the time goes in v5:
time: 57.3 us; the launch traced here: 57.1 us
  blocking collectives  40.8 us (71%)
  Pallas kernels  13.9 us (24%)
  local copies, waits for them, and re-layouts  1.77 us (3%)
    all_to_all x1, blocking collectives, window_local(): pieces = lax.all_to_all(pieces, ('rows', 'tm'), 0, 0, tiled=True)  29.8 us
    all_to_all x1, blocking collectives, window_local(): out = lax.all_to_all(out, ('rows', 'tm'), 0, 0, tiled=True)  11.1 us
    pallas_call x1, Pallas kernels, encode_window(): pl.pallas_call(functools.partial(encode_kernel, plan), out_shape=jax.Shap...  10.9 us
    unnamed x24, local copies, waits for them, and re-layouts  1.77 us
    pallas_call x1, Pallas kernels, pack(): pl.pallas_call(functools.partial(pack_kernel, plan), out_shape=jax.ShapeD...  1.39 us
  transfers between devices with their start and end apart: 1, of which 0 were waited for; matrix products, arithmetic and copies ran while one was open for 0% of the time, Pallas kernels for 1%

profile of v5, /device:TPU:0, one launch (start us, length us, event | category | flops | bytes accessed | tf_op | source)
XLA Modules:
  0.0 57.1 jit_solution(17161726030587262700)
XLA Ops:
  0.0 0.5 collective-permute-start
  0.5 0.0 copy-start.2
  0.5 1.1 %copy-done.2 = bf16[4,4,2,9984]{3,2,1,0:T(2,128)(2,1)S(1)} copy-done((bf16[4,4,2,9984]{3,2,1,0:T(2,128)(2,1)S(1)}, bf16[4,4,2,9984]{3,2,1,0:T(2,128)(2,1)}, u32[]{:S(2)}) %copy-start.2) | copy-done | bytes 639000
  1.5 0.0 copy-start.7
  1.5 0.0 copy-start.8
  1.5 0.0 copy-start.9
  1.5 0.0 copy-start.10
  1.5 0.0 copy-start.11
  1.6 0.2 shard_map.119.mine_ref
  1.8 0.0 copy-start.4
  1.8 0.0 copy-start.5
  1.8 0.0 copy-start.6
  1.8 0.4 copy-done.7
  2.2 0.0 copy-done.8
  2.2 0.0 copy-done.9
  2.2 0.0 copy-done.10
  2.2 0.0 copy-done.11
  2.3 0.2 copy-done.4
  2.4 0.0 copy-done.5
  2.4 0.0 copy-done.6
  2.5 0.6 shard_map.118.vector_ref
  3.0 0.0 collective-permute-done.other_ref
  3.0 1.4 %shard_map.120 = bf16[16,8,3072]{2,1,0:T(8,128)(2,1)S(1)} custom-call(s32[8]{0:T(128)S(1)} %copy-done.4, s32[8]{0:T(128)S(1)} %copy-done.5, f32[8,128]{1,0:T(8,128)S(1)} %shard_map.118.vector_ref, bf16[4,4,2,9984]{3,2,1,0:T(2,128)(2,1)S(1)} %shard_map.119.mine_ref, bf16[4,4,2,9984]{3,2,1,0:T(2,128)(2,1)S(1)} %collective-permute-done.other_ref), custom_call_target="tpu_custom_call" | custom-call | tf_op jit(solution)/shard_map/pallas_call | solution.py:343
  4.4 0.0 copy-start
  4.4 0.0 copy-start.1
  4.5 0.0 copy-start.3
  4.5 29.8 %all_to_all.10.pieces_ref = bf16[16,8,3072]{2,1,0:T(8,128)(2,1)S(1)} all-to-all(bf16[16,8,3072]{2,1,0:T(8,128)(2,1)S(1)} %shard_map.120), channel_id=1, replica_groups=mesh['tm'=4,'rows'=4,'clip'=2] {'rows','tm'}, dimensions={0} | all-to-all | bytes 1572864 | tf_op jit(solution)/shard_map/all_to_all | solution.py:683
  34.2 0.0 copy-done
  34.2 0.0 copy-done.1
  34.2 0.0 copy-done.3
  34.2 10.9 %shard_map.121 = bf16[16,4,1280]{2,1,0:T(4,128)(2,1)S(1)} custom-call(bf16[16,8,3072]{2,1,0:T(8,128)(2,1)S(1)} %all_to_all.10.pieces_ref, f32[8,128]{1,0:T(8,128)S(1)} %shard_map.118.vector_ref, bf16[27,96,96]{2,1,0:T(8,128)(2,1)S(1)} %bitcast.11, bf16[27,96,96]{2,1,0:T(8,128)(2,1)S(1)} %bitcast.12, bf16[9,96,96]{2,1,0:T(8,128)(2,1)S(1)} %bitcast.13), custom_call_target="tpu_custom_call" | custom-call | tf_op jit(solution)/shard_map/pallas_call | solution.py:645
  45.2 11.1 %all_to_all.11.pieces_ref = bf16[16,4,1280]{2,1,0:T(4,128)(2,1)S(1)} all-to-all(bf16[16,4,1280]{2,1,0:T(4,128)(2,1)S(1)} %shard_map.121), channel_id=1, replica_groups=mesh['tm'=4,'rows'=4,'clip'=2] {'rows','tm'}, dimensions={0} | all-to-all | bytes 327680 | tf_op jit(solution)/shard_map/all_to_all | solution.py:685
  56.3 0.8 %shard_map.122 = bf16[4,4,4992]{2,1,0:T(4,128)(2,1)} custom-call(bf16[16,4,1280]{2,1,0:T(4,128)(2,1)S(1)} %all_to_all.11.pieces_ref), custom_call_target="tpu_custom_call" | custom-call | tf_op jit(solution)/shard_map/pallas_call | solution.py:380
Async XLA Ops:
  0.0 3.0 %collective-permute-start = (bf16[4,4,2,9984]{3,2,1,0:T(2,128)(2,1)}, bf16[4,4,2,9984]{3,2,1,0:T(2,128)(2,1)S(1)}, u32[]{:S(2)}, u32[]{:S(2)}) collective-permute-start(bf16[4,4,2,9984]{3,2,1,0:T(2,128)(2,1)} %source_ref.1), channel_id=1, source_target_pairs={{0,1},{1,0},{2,3},{3,2},{4,5},{5,4},{6,7},{7,6},{8,9},{9,8},{10,11... | collective-permute-start | bytes 1916936 | tf_op jit(solution)/shard_map/ppermute | solution.py:678
  0.5 1.1 %copy-start.2 = (bf16[4,4,2,9984]{3,2,1,0:T(2,128)(2,1)S(1)}, bf16[4,4,2,9984]{3,2,1,0:T(2,128)(2,1)}, u32[]{:S(2)}) copy-start(bf16[4,4,2,9984]{3,2,1,0:T(2,128)(2,1)} %source_ref.1) | copy-start | bytes 1916932
  1.5 0.7 %copy-start.7 = (f32[96]{0:T(128)S(1)}, f32[96]{0:T(128)}, u32[]{:S(2)}) copy-start(f32[96]{0:T(128)} %param.16) | copy-start | bytes 1156
  1.5 0.7 %copy-start.8 = (f32[96]{0:T(128)S(1)}, f32[96]{0:T(128)}, u32[]{:S(2)}) copy-start(f32[96]{0:T(128)} %param.18) | copy-start | bytes 1156
  1.5 0.7 %copy-start.9 = (f32[96]{0:T(128)S(1)}, f32[96]{0:T(128)}, u32[]{:S(2)}) copy-start(f32[96]{0:T(128)} %param.19) | copy-start | bytes 1156
  1.5 0.7 %copy-start.10 = (f32[96]{0:T(128)S(1)}, f32[96]{0:T(128)}, u32[]{:S(2)}) copy-start(f32[96]{0:T(128)} %param.21) | copy-start | bytes 1156
  1.5 0.7 %copy-start.11 = (f32[96]{0:T(128)S(1)}, f32[96]{0:T(128)}, u32[]{:S(2)}) copy-start(f32[96]{0:T(128)} %param.23) | copy-start | bytes 1156
  1.8 0.7 %copy-start.4 = (s32[8]{0:T(128)S(1)}, s32[8]{0:T(128)}, u32[]{:S(2)}) copy-start(s32[8]{0:T(128)} %stored_ref.3) | copy-start | bytes 100
  1.8 0.7 %copy-start.5 = (s32[8]{0:T(128)S(1)}, s32[8]{0:T(128)}, u32[]{:S(2)}) copy-start(s32[8]{0:T(128)} %owner_ref.3) | copy-start | bytes 100
  1.8 0.7 %copy-start.6 = (s32[8]{0:T(128)S(1)}, s32[8]{0:T(128)}, u32[]{:S(2)}) copy-start(s32[8]{0:T(128)} %lengths_ref.1) | copy-start | bytes 100
  4.4 29.8 %copy-start = (bf16[3,3,3,96,96]{4,3,2,1,0:T(8,128)(2,1)S(1)}, bf16[3,3,3,96,96]{4,3,2,1,0:T(8,128)(2,1)}, u32[]{:S(2)}) copy-start(bf16[3,3,3,96,96]{4,3,2,1,0:T(8,128)(2,1)} %param.17) | copy-start | bytes 1492996
  4.4 29.8 %copy-start.1 = (bf16[3,3,3,96,96]{4,3,2,1,0:T(8,128)(2,1)S(1)}, bf16[3,3,3,96,96]{4,3,2,1,0:T(8,128)(2,1)}, u32[]{:S(2)}) copy-start(bf16[3,3,3,96,96]{4,3,2,1,0:T(8,128)(2,1)} %param.20) | copy-start | bytes 1492996
  4.5 29.8 %copy-start.3 = (bf16[3,3,96,96]{3,2,1,0:T(8,128)(2,1)S(1)}, bf16[3,3,96,96]{3,2,1,0:T(8,128)(2,1)}, u32[]{:S(2)}) copy-start(bf16[3,3,96,96]{3,2,1,0:T(8,128)(2,1)} %param.22) | copy-start | bytes 497668

commit v6 on v5

--- a/solution.py
+++ b/solution.py
@@ -507,7 +507,7 @@
                     )
                     moved = jnp.where(row_in_tile >= shift, turned, ahead)
                 act_ref[
-                    2 - shift, pair, 1 : height + 1, :, tile * LANES : (tile + 1) * LANES
+                    2 - shift, pair, 0:height, :, tile * LANES : (tile + 1) * LANES
                 ] = moved.astype(jnp.bfloat16).reshape(height, frames, LANES)
 
     def both(row):
@@ -518,20 +518,21 @@
     second_weights = slice(conv_rows, reduce_rows)
 
     def convolve(act_ref, weights, first_pair, count):
-        parts = [
-            act_ref[
-                tap // 3, first_pair : first_pair + count, tap % 3 : tap % 3 + height
-            ].reshape(
-                count * rows, 3 * LANES
-            )
-            for tap in range(9)
-        ]
+        parts = []
+        for tap in range(9):
+            chosen = act_ref.at[tap // 3, first_pair : first_pair + count]
+            if tap % 3 == 0:
+                window = jnp.concatenate(
+                    [chosen[:, height : height + 1], chosen[:, 0 : height - 1]], axis=1
+                )
+            else:
+                window = chosen[:, tap % 3 - 1 : tap % 3 - 1 + height]
+            parts.append(window.reshape(count * rows, 3 * LANES))
         stack = jnp.concatenate(parts, axis=1)
         return jnp.dot(stack, weights_ref[weights], preferred_element_type=jnp.float32)
 
     for act_ref in (act_first_ref, act_second_ref):
-        act_ref[:, :, 0] = jnp.zeros_like(act_ref[:, :, 0])
-        act_ref[:, :, height + 1] = jnp.zeros_like(act_ref[:, :, height + 1])
+        act_ref[:, :, height] = jnp.zeros_like(act_ref[:, :, height])
     wide_first_ref[0] = jnp.zeros_like(wide_first_ref[0])
     wide_second_ref[pairs] = jnp.zeros_like(wide_second_ref[pairs])
     block_ref[:, height] = jnp.zeros_like(block_ref[:, height])
@@ -640,7 +641,7 @@
     rows = plan.height * plan.all_frames
     out_tiles = -(-plan.own // 2 * channels // LANES)
     vmem = pl.BlockSpec(memory_space=pltpu.VMEM)
-    acts = pltpu.VMEM((3, pairs, plan.height + 2, plan.all_frames, 3 * LANES), jnp.bfloat16)
+    acts = pltpu.VMEM((3, pairs, plan.height + 1, plan.all_frames, 3 * LANES), jnp.bfloat16)
     wide = pltpu.VMEM((pairs + 2, rows, 2 * LANES), jnp.float32)
     return pl.pallas_call(
         functools.partial(encode_kernel, plan),

time: 57.3 us -> 57.3 us (level)
  no operation moved by 1% of the time
where the time goes in v6:
time: 57.3 us; the launch traced here: 57 us
  blocking collectives  40.8 us (71%)
  Pallas kernels  13.8 us (24%)
  local copies, waits for them, and re-layouts  1.77 us (3%)
    all_to_all x1, blocking collectives, window_local(): pieces = lax.all_to_all(pieces, ('rows', 'tm'), 0, 0, tiled=True)  29.7 us
    all_to_all x1, blocking collectives, window_local(): out = lax.all_to_all(out, ('rows', 'tm'), 0, 0, tiled=True)  11.1 us
    pallas_call x1, Pallas kernels, encode_window(): pl.pallas_call(functools.partial(encode_kernel, plan), out_shape=jax.Shap...  10.9 us
    unnamed x24, local copies, waits for them, and re-layouts  1.77 us
    pallas_call x1, Pallas kernels, pack(): pl.pallas_call(functools.partial(pack_kernel, plan), out_shape=jax.ShapeD...  1.39 us
  transfers between devices with their start and end apart: 1, of which 0 were waited for; matrix products, arithmetic and copies ran while one was open for 0% of the time, Pallas kernels for 1%

profile of v6, /device:TPU:0, one launch (start us, length us, event | category | flops | bytes accessed | tf_op | source)
XLA Modules:
  0.0 57.0 jit_solution(11640161147378975845)
XLA Ops:
  0.0 0.5 collective-permute-start
  0.5 0.0 copy-start.2
  0.5 1.1 %copy-done.2 = bf16[4,4,2,9984]{3,2,1,0:T(2,128)(2,1)S(1)} copy-done((bf16[4,4,2,9984]{3,2,1,0:T(2,128)(2,1)S(1)}, bf16[4,4,2,9984]{3,2,1,0:T(2,128)(2,1)}, u32[]{:S(2)}) %copy-start.2) | copy-done | bytes 639000
  1.5 0.0 copy-start.7
  1.5 0.0 copy-start.8
  1.5 0.0 copy-start.9
  1.5 0.0 copy-start.10
  1.5 0.0 copy-start.11
  1.6 0.2 shard_map.119.mine_ref
  1.8 0.0 copy-start.4
  1.8 0.0 copy-start.5
  1.8 0.0 copy-start.6
  1.8 0.4 copy-done.7
  2.2 0.0 copy-done.8
  2.2 0.0 copy-done.9
  2.2 0.0 copy-done.10
  2.2 0.0 copy-done.11
  2.3 0.2 copy-done.4
  2.4 0.0 copy-done.5
  2.4 0.0 copy-done.6
  2.5 0.6 shard_map.118.vector_ref
  3.0 0.0 collective-permute-done.other_ref
  3.0 1.4 %shard_map.120 = bf16[16,8,3072]{2,1,0:T(8,128)(2,1)S(1)} custom-call(s32[8]{0:T(128)S(1)} %copy-done.4, s32[8]{0:T(128)S(1)} %copy-done.5, f32[8,128]{1,0:T(8,128)S(1)} %shard_map.118.vector_ref, bf16[4,4,2,9984]{3,2,1,0:T(2,128)(2,1)S(1)} %shard_map.119.mine_ref, bf16[4,4,2,9984]{3,2,1,0:T(2,128)(2,1)S(1)} %collective-permute-done.other_ref), custom_call_target="tpu_custom_call" | custom-call | tf_op jit(solution)/shard_map/pallas_call | solution.py:343
  4.4 0.0 copy-start
  4.4 0.0 copy-start.1
  4.5 0.0 copy-start.3
  4.5 29.7 %all_to_all.10.pieces_ref = bf16[16,8,3072]{2,1,0:T(8,128)(2,1)S(1)} all-to-all(bf16[16,8,3072]{2,1,0:T(8,128)(2,1)S(1)} %shard_map.120), channel_id=1, replica_groups=mesh['tm'=4,'rows'=4,'clip'=2] {'rows','tm'}, dimensions={0} | all-to-all | bytes 1572864 | tf_op jit(solution)/shard_map/all_to_all | solution.py:684
  34.2 0.0 copy-done
  34.2 0.0 copy-done.1
  34.2 0.0 copy-done.3
  34.2 10.9 %shard_map.121 = bf16[16,4,1280]{2,1,0:T(4,128)(2,1)S(1)} custom-call(bf16[16,8,3072]{2,1,0:T(8,128)(2,1)S(1)} %all_to_all.10.pieces_ref, f32[8,128]{1,0:T(8,128)S(1)} %shard_map.118.vector_ref, bf16[27,96,96]{2,1,0:T(8,128)(2,1)S(1)} %bitcast.11, bf16[27,96,96]{2,1,0:T(8,128)(2,1)S(1)} %bitcast.12, bf16[9,96,96]{2,1,0:T(8,128)(2,1)S(1)} %bitcast.13), custom_call_target="tpu_custom_call" | custom-call | tf_op jit(solution)/shard_map/pallas_call | solution.py:646
  45.1 11.1 %all_to_all.11.pieces_ref = bf16[16,4,1280]{2,1,0:T(4,128)(2,1)S(1)} all-to-all(bf16[16,4,1280]{2,1,0:T(4,128)(2,1)S(1)} %shard_map.121), channel_id=1, replica_groups=mesh['tm'=4,'rows'=4,'clip'=2] {'rows','tm'}, dimensions={0} | all-to-all | bytes 327680 | tf_op jit(solution)/shard_map/all_to_all | solution.py:686
  56.2 0.8 %shard_map.122 = bf16[4,4,4992]{2,1,0:T(4,128)(2,1)} custom-call(bf16[16,4,1280]{2,1,0:T(4,128)(2,1)S(1)} %all_to_all.11.pieces_ref), custom_call_target="tpu_custom_call" | custom-call | tf_op jit(solution)/shard_map/pallas_call | solution.py:380
Async XLA Ops:
  0.0 3.0 %collective-permute-start = (bf16[4,4,2,9984]{3,2,1,0:T(2,128)(2,1)}, bf16[4,4,2,9984]{3,2,1,0:T(2,128)(2,1)S(1)}, u32[]{:S(2)}, u32[]{:S(2)}) collective-permute-start(bf16[4,4,2,9984]{3,2,1,0:T(2,128)(2,1)} %source_ref.1), channel_id=1, source_target_pairs={{0,1},{1,0},{2,3},{3,2},{4,5},{5,4},{6,7},{7,6},{8,9},{9,8},{10,11... | collective-permute-start | bytes 1916936 | tf_op jit(solution)/shard_map/ppermute | solution.py:679
  0.5 1.1 %copy-start.2 = (bf16[4,4,2,9984]{3,2,1,0:T(2,128)(2,1)S(1)}, bf16[4,4,2,9984]{3,2,1,0:T(2,128)(2,1)}, u32[]{:S(2)}) copy-start(bf16[4,4,2,9984]{3,2,1,0:T(2,128)(2,1)} %source_ref.1) | copy-start | bytes 1916932
  1.5 0.7 %copy-start.7 = (f32[96]{0:T(128)S(1)}, f32[96]{0:T(128)}, u32[]{:S(2)}) copy-start(f32[96]{0:T(128)} %param.16) | copy-start | bytes 1156
  1.5 0.7 %copy-start.8 = (f32[96]{0:T(128)S(1)}, f32[96]{0:T(128)}, u32[]{:S(2)}) copy-start(f32[96]{0:T(128)} %param.18) | copy-start | bytes 1156
  1.5 0.7 %copy-start.9 = (f32[96]{0:T(128)S(1)}, f32[96]{0:T(128)}, u32[]{:S(2)}) copy-start(f32[96]{0:T(128)} %param.19) | copy-start | bytes 1156
  1.5 0.7 %copy-start.10 = (f32[96]{0:T(128)S(1)}, f32[96]{0:T(128)}, u32[]{:S(2)}) copy-start(f32[96]{0:T(128)} %param.21) | copy-start | bytes 1156
  1.5 0.7 %copy-start.11 = (f32[96]{0:T(128)S(1)}, f32[96]{0:T(128)}, u32[]{:S(2)}) copy-start(f32[96]{0:T(128)} %param.23) | copy-start | bytes 1156
  1.8 0.7 %copy-start.4 = (s32[8]{0:T(128)S(1)}, s32[8]{0:T(128)}, u32[]{:S(2)}) copy-start(s32[8]{0:T(128)} %stored_ref.3) | copy-start | bytes 100
  1.8 0.7 %copy-start.5 = (s32[8]{0:T(128)S(1)}, s32[8]{0:T(128)}, u32[]{:S(2)}) copy-start(s32[8]{0:T(128)} %owner_ref.3) | copy-start | bytes 100
  1.8 0.7 %copy-start.6 = (s32[8]{0:T(128)S(1)}, s32[8]{0:T(128)}, u32[]{:S(2)}) copy-start(s32[8]{0:T(128)} %lengths_ref.1) | copy-start | bytes 100
  4.4 29.8 %copy-start = (bf16[3,3,3,96,96]{4,3,2,1,0:T(8,128)(2,1)S(1)}, bf16[3,3,3,96,96]{4,3,2,1,0:T(8,128)(2,1)}, u32[]{:S(2)}) copy-start(bf16[3,3,3,96,96]{4,3,2,1,0:T(8,128)(2,1)} %param.17) | copy-start | bytes 1492996
  4.4 29.8 %copy-start.1 = (bf16[3,3,3,96,96]{4,3,2,1,0:T(8,128)(2,1)S(1)}, bf16[3,3,3,96,96]{4,3,2,1,0:T(8,128)(2,1)}, u32[]{:S(2)}) copy-start(bf16[3,3,3,96,96]{4,3,2,1,0:T(8,128)(2,1)} %param.20) | copy-start | bytes 1492996
  4.5 29.8 %copy-start.3 = (bf16[3,3,96,96]{3,2,1,0:T(8,128)(2,1)S(1)}, bf16[3,3,96,96]{3,2,1,0:T(8,128)(2,1)}, u32[]{:S(2)}) copy-start(bf16[3,3,96,96]{3,2,1,0:T(8,128)(2,1)} %param.22) | copy-start | bytes 497668
